TPU v7x, 128 devices: a whole 4x4x4 slice. The times are simulated.
128 devices in a mesh: dp: 32 (over y, x_hi, z), seq: 4 (over x_lo, core).
Axes of the slice: x: 4 (x_hi: 2, x_lo: 2; x = x_hi * 2 + x_lo), y: 4, z: 4, core: 2. Of those that a mesh axis runs over, the one named last changes fastest.
Arguments:
- tokens: bfloat16 [32, 512, 512], P('dp', 'seq'), may hold values from -6 to 6
- cotangent: bfloat16 [32, 512, 512], P('dp', 'seq'), may hold values from -6 to 6
- segments: int32 [32, 512], P('dp', 'seq'), may hold values from 0 to 2, as said below
- w_attn: float32 [2, 512, 2048], P(None, ('dp', 'seq')), may hold values from -1.06066017 to 1.06066017
- w_mlp: float32 [2, 512, 4096], P(None, ('dp', 'seq')), may hold values from -0.26516504 to 0.26516504
- vectors: float32 [2, 12, 512], P(None, None, ('dp', 'seq')), may hold values from -1.2 to 1.5
- m_attn: float32 [2, 512, 2048], P(None, ('dp', 'seq')), may hold values from -16 to 16
- m_mlp: float32 [2, 512, 4096], P(None, ('dp', 'seq')), may hold values from -16 to 16
- m_vec: float32 [2, 12, 512], P(None, None, ('dp', 'seq')), may hold values from -16 to 16
- v_attn: float32 [2, 512, 2048], P(None, ('dp', 'seq')), may hold values from 0.049152 to 4.9152
- v_mlp: float32 [2, 512, 4096], P(None, ('dp', 'seq')), may hold values from 0.049152 to 4.9152
- v_vec: float32 [2, 12, 512], P(None, None, ('dp', 'seq')), may hold values from 0.049152 to 4.9152
Outputs:
- block_out: bfloat16 [32, 512, 512], P('dp', 'seq')
- input_grad: float32 [32, 512, 512], P('dp', 'seq')
- attn_first: float32 [2, 512, 2048], P(None, ('dp', 'seq'))
- attn_second: float32 [2, 512, 2048], P(None, ('dp', 'seq'))
- attn_new: float32 [2, 512, 2048], P(None, ('dp', 'seq'))
- mlp_first: float32 [2, 512, 4096], P(None, ('dp', 'seq'))
- mlp_second: float32 [2, 512, 4096], P(None, ('dp', 'seq'))
- mlp_new: float32 [2, 512, 4096], P(None, ('dp', 'seq'))
- vec_first: float32 [2, 12, 512], P(None, None, ('dp', 'seq'))
- vec_second: float32 [2, 12, 512], P(None, None, ('dp', 'seq'))
- vec_new: float32 [2, 12, 512], P(None, None, ('dp', 'seq'))
Inputs may be any that keep to these rules, and one draw needn't show every extreme that they name: `segments`: each sequence holds exactly three documents numbered 0, 1, 2 in order of position; document 1 covers more than three quarters of the sequence.
All inputs are finite; a program needn't handle non-finite values.
Results may differ from a plain program's by a relative error of at most 0.04.
Values may be sent and summed in bfloat16 or wider, within the bound.
A program may use at most 192 MiB of HBM per device.

v0:
```python
import jax
import jax.numpy as jnp
from jax import lax
from jax.sharding import PartitionSpec as P

HD = 64
STEP = 10


NORM_EPSILON = 1e-06
ADAM_EPSILON = 1e-06
BETA_FIRST = 0.9
BETA_SECOND = 0.999
LEARN_RATE = 0.03
VECTOR_RATE = 0.2
WEIGHT_DECAY = 0.01
MASKED_SCORE = -1e30


def layer_norm(summed, gain, shift):
    center = summed - jnp.mean(summed, axis=-1, keepdims=True)
    spread = jnp.mean(center * center, axis=-1, keepdims=True)
    return center * lax.rsqrt(spread + NORM_EPSILON) * gain + shift


def exact_gelu(values):
    return jax.nn.gelu(values, approximate=False)


def norm_back(summed, gain, shift, grad_out):
    unused_out, pullback = jax.vjp(layer_norm, summed, gain, shift)
    return pullback(grad_out)


def split_heads(values):
    seq_count, row_count, model_width = values.shape
    return values.reshape(seq_count, row_count, model_width // HD, HD)


def attend_scores(queries, keys_full, same_doc):
    raw = jnp.einsum(
        "sqhd,skhd->shqk",
        split_heads(queries),
        split_heads(keys_full),
        preferred_element_type=jnp.float32,
    ) * HD ** (-0.5)
    return jnp.where(same_doc[:, None], raw, MASKED_SCORE)


def forward_layer(hidden_state, attn_weights, mlp_weights, vec_layer, same_doc):
    seq_count, row_count, model_width = hidden_state.shape
    hidden = mlp_weights.shape[1] // 2
    inner_rows = hidden // model_width
    low_in = hidden_state.astype(jnp.bfloat16)
    projected = jnp.einsum(
        "std,de->ste",
        low_in,
        attn_weights[:, : 3 * model_width],
        preferred_element_type=jnp.float32,
    )
    queries = (projected[..., :model_width] + vec_layer[0]).astype(jnp.bfloat16)
    key_local = projected[..., model_width : 2 * model_width].astype(jnp.bfloat16)
    value_local = (projected[..., 2 * model_width :] + vec_layer[1]).astype(jnp.bfloat16)
    keys_full, values_full = (
        lax.all_gather(key_local, "seq", axis=1, tiled=True),
        lax.all_gather(value_local, "seq", axis=1, tiled=True),
    )
    scores = attend_scores(queries, keys_full, same_doc)
    top_score = jnp.max(scores, axis=-1, keepdims=True)
    exp_scores = jnp.exp(scores - top_score)
    exp_total = jnp.sum(exp_scores, axis=-1, keepdims=True)
    attn_probs = (exp_scores / exp_total).astype(jnp.bfloat16)
    log_total = top_score + jnp.log(exp_total)
    mixed_low = (
        jnp.einsum(
            "shqk,skhd->sqhd",
            attn_probs,
            split_heads(values_full),
            preferred_element_type=jnp.float32,
        )
        .reshape(hidden_state.shape)
        .astype(jnp.bfloat16)
    )
    attn_out = (
        jnp.einsum(
            "ste,ed->std",
            mixed_low,
            attn_weights[:, 3 * model_width :],
            preferred_element_type=jnp.float32,
        )
        + vec_layer[2]
    )
    first_sum = hidden_state + attn_out
    normed = layer_norm(first_sum, vec_layer[3], vec_layer[4])
    normed_low = normed.astype(jnp.bfloat16)
    in_bias = vec_layer[5 : 5 + inner_rows].reshape(hidden)
    pre_act = (
        jnp.einsum(
            "std,df->stf", normed_low, mlp_weights[:, :hidden], preferred_element_type=jnp.float32
        )
        + in_bias
    )
    activ_low = exact_gelu(pre_act).astype(jnp.bfloat16)
    back_out = (
        jnp.einsum(
            "stf,df->std", activ_low, mlp_weights[:, hidden:], preferred_element_type=jnp.float32
        )
        + vec_layer[5 + inner_rows]
    )
    second_sum = normed + back_out
    result = layer_norm(second_sum, vec_layer[6 + inner_rows], vec_layer[7 + inner_rows])
    saved_layer = (
        low_in,
        queries,
        keys_full,
        values_full,
        key_local,
        value_local,
        log_total,
        mixed_low,
        first_sum,
        normed_low,
        pre_act,
        activ_low,
        second_sum,
    )
    return (result, saved_layer)


def backward_layer(grad_state, saved_layer, attn_weights, mlp_weights, vec_layer, same_doc):
    (
        low_in,
        queries,
        keys_full,
        values_full,
        key_local,
        value_local,
        log_total,
        mixed_low,
        first_sum,
        normed_low,
        pre_act,
        activ_low,
        second_sum,
    ) = saved_layer
    seq_count, row_count, model_width = grad_state.shape
    hidden = mlp_weights.shape[1] // 2
    inner_rows = hidden // model_width
    grad_second, grad_gain_two, grad_shift_two = norm_back(
        second_sum, vec_layer[6 + inner_rows], vec_layer[7 + inner_rows], grad_state
    )
    grad_outbias = jnp.sum(grad_second, axis=(0, 1))
    grad_back_low = grad_second.astype(jnp.bfloat16)
    grad_w_out = jnp.einsum(
        "std,stf->df", grad_back_low, activ_low, preferred_element_type=jnp.float32
    )
    grad_activ = jnp.einsum(
        "std,df->stf", grad_back_low, mlp_weights[:, hidden:], preferred_element_type=jnp.float32
    )
    unused_act, gelu_pull = jax.vjp(exact_gelu, pre_act)
    grad_pre_low = gelu_pull(grad_activ)[0].astype(jnp.bfloat16)
    grad_inbias = jnp.sum(grad_pre_low.astype(jnp.float32), axis=(0, 1))
    grad_w_in = jnp.einsum(
        "std,stf->df", normed_low, grad_pre_low, preferred_element_type=jnp.float32
    )
    grad_normed = grad_second + jnp.einsum(
        "stf,df->std", grad_pre_low, mlp_weights[:, :hidden], preferred_element_type=jnp.float32
    )
    grad_first, grad_gain_one, grad_shift_one = norm_back(
        first_sum, vec_layer[3], vec_layer[4], grad_normed
    )
    grad_obias = jnp.sum(grad_first, axis=(0, 1))
    grad_attn_low = grad_first.astype(jnp.bfloat16)
    grad_w_o = jnp.einsum(
        "ste,std->ed", mixed_low, grad_attn_low, preferred_element_type=jnp.float32
    )
    grad_mixed_low = jnp.einsum(
        "std,ed->ste",
        grad_attn_low,
        attn_weights[:, 3 * model_width :],
        preferred_element_type=jnp.float32,
    ).astype(jnp.bfloat16)
    key_rows = keys_full.shape[1]
    scores = attend_scores(queries, keys_full, same_doc)
    attn_probs = jnp.exp(scores - log_total)
    grad_heads = split_heads(grad_mixed_low)
    grad_probs = jnp.einsum(
        "sqhd,skhd->shqk", grad_heads, split_heads(values_full), preferred_element_type=jnp.float32
    )
    grad_values = jnp.einsum(
        "shqk,sqhd->skhd",
        attn_probs.astype(jnp.bfloat16),
        grad_heads,
        preferred_element_type=jnp.float32,
    ).reshape(seq_count, key_rows, model_width)
    row_dot = jnp.sum(grad_probs * attn_probs, axis=-1, keepdims=True)
    grad_scores_low = (attn_probs * (grad_probs - row_dot)).astype(jnp.bfloat16)
    score_scale = HD ** (-0.5)
    grad_queries_low = (
        (
            jnp.einsum(
                "shqk,skhd->sqhd",
                grad_scores_low,
                split_heads(keys_full),
                preferred_element_type=jnp.float32,
            )
            * score_scale
        )
        .reshape(grad_state.shape)
        .astype(jnp.bfloat16)
    )
    grad_keys = (
        jnp.einsum(
            "shqk,sqhd->skhd",
            grad_scores_low,
            split_heads(queries),
            preferred_element_type=jnp.float32,
        ).reshape(seq_count, key_rows, model_width)
        * score_scale
    )
    grad_key_sum, grad_value_sum = (
        lax.psum_scatter(
            grad_keys.astype(jnp.bfloat16), "seq", scatter_dimension=1, tiled=True
        ).astype(jnp.float32),
        lax.psum_scatter(
            grad_values.astype(jnp.bfloat16), "seq", scatter_dimension=1, tiled=True
        ).astype(jnp.float32),
    )
    grad_key_low = grad_key_sum.astype(jnp.bfloat16)
    grad_value_low = grad_value_sum.astype(jnp.bfloat16)
    grad_proj = jnp.concatenate([grad_queries_low, grad_key_low, grad_value_low], axis=-1)
    grad_w_qkv = jnp.einsum("std,ste->de", low_in, grad_proj, preferred_element_type=jnp.float32)
    grad_input = grad_first + jnp.einsum(
        "ste,de->std",
        grad_proj,
        attn_weights[:, : 3 * model_width],
        preferred_element_type=jnp.float32,
    )
    grad_qbias = jnp.sum(grad_queries_low.astype(jnp.float32), axis=(0, 1))
    grad_vbias = jnp.sum(grad_value_low.astype(jnp.float32), axis=(0, 1))
    vec_grad = jnp.concatenate(
        [
            jnp.stack([grad_qbias, grad_vbias, grad_obias, grad_gain_one, grad_shift_one]),
            grad_inbias.reshape(inner_rows, model_width),
            jnp.stack([grad_outbias, grad_gain_two, grad_shift_two]),
        ],
        axis=0,
    )
    layer_grads = (
        jnp.concatenate([grad_w_qkv, grad_w_o], axis=1),
        jnp.concatenate([grad_w_in, grad_w_out], axis=1),
        vec_grad,
    )
    return (grad_input, layer_grads)


def reduce_grads(grad_attn, grad_mlp, grad_vec):
    vec_cols = grad_vec.T
    own_attn, own_mlp, own_vec = (
        lax.psum_scatter(grad_attn, ("dp", "seq"), scatter_dimension=0, tiled=True),
        lax.psum_scatter(grad_mlp, ("dp", "seq"), scatter_dimension=0, tiled=True),
        lax.psum_scatter(vec_cols, ("dp", "seq"), scatter_dimension=0, tiled=True),
    )
    return (own_attn, own_mlp, own_vec.T)


def adam_update(weight, grad, first, second, rate, decay):
    first_new = BETA_FIRST * first + (1.0 - BETA_FIRST) * grad
    second_new = BETA_SECOND * second + (1.0 - BETA_SECOND) * grad * grad
    first_fix = 1.0 - BETA_FIRST**STEP
    second_fix = 1.0 - BETA_SECOND**STEP
    weight_new = weight - rate * (
        first_new / first_fix / (jnp.sqrt(second_new / second_fix) + ADAM_EPSILON) + decay * weight
    )
    return (first_new, second_new, weight_new)


def local(
    tokens, cotangent, segments, w_attn, w_mlp, vectors, m_attn, m_mlp, m_vec, v_attn, v_mlp, v_vec
):
    gathered_attn, gathered_mlp, gathered_vec = (
        lax.all_gather(w_attn.astype(jnp.bfloat16), ("dp", "seq"), axis=1, tiled=True),
        lax.all_gather(w_mlp.astype(jnp.bfloat16), ("dp", "seq"), axis=1, tiled=True),
        lax.all_gather(vectors.astype(jnp.bfloat16), ("dp", "seq"), axis=2, tiled=True),
    )
    key_docs = lax.all_gather(segments, "seq", axis=1, tiled=True)
    same_doc = segments[:, :, None] == key_docs[:, None, :]
    layer_count = w_attn.shape[0]
    vec_float = gathered_vec.astype(jnp.float32)
    hidden_state = tokens.astype(jnp.float32)
    saved_all = []
    for layer_index in range(layer_count):
        hidden_state, saved_layer = forward_layer(
            hidden_state,
            gathered_attn[layer_index],
            gathered_mlp[layer_index],
            vec_float[layer_index],
            same_doc,
        )
        saved_all.append(saved_layer)
    block_out = hidden_state.astype(jnp.bfloat16)
    grad_state = cotangent.astype(jnp.float32)
    shard_grads = [None] * layer_count
    for layer_index in reversed(range(layer_count)):
        grad_state, layer_grads = backward_layer(
            grad_state,
            saved_all[layer_index],
            gathered_attn[layer_index],
            gathered_mlp[layer_index],
            vec_float[layer_index],
            same_doc,
        )
        shard_grads[layer_index] = reduce_grads(*layer_grads)
    grad_attn = jnp.stack([entry_grads[0] for entry_grads in shard_grads])
    grad_mlp = jnp.stack([entry_grads[1] for entry_grads in shard_grads])
    grad_vec = jnp.stack([entry_grads[2] for entry_grads in shard_grads])
    attn_first, attn_second, attn_new = adam_update(
        w_attn, grad_attn, m_attn, v_attn, LEARN_RATE, WEIGHT_DECAY
    )
    mlp_first, mlp_second, mlp_new = adam_update(
        w_mlp, grad_mlp, m_mlp, v_mlp, LEARN_RATE, WEIGHT_DECAY
    )
    vec_first, vec_second, vec_new = adam_update(vectors, grad_vec, m_vec, v_vec, VECTOR_RATE, 0.0)
    return (
        block_out,
        grad_state,
        attn_first,
        attn_second,
        attn_new,
        mlp_first,
        mlp_second,
        mlp_new,
        vec_first,
        vec_second,
        vec_new,
    )


def solution(mesh):
    in_specs = (
        P("dp", "seq", None),
        P("dp", "seq", None),
        P("dp", "seq"),
        P(None, ("dp", "seq"), None),
        P(None, ("dp", "seq"), None),
        P(None, None, ("dp", "seq")),
        P(None, ("dp", "seq"), None),
        P(None, ("dp", "seq"), None),
        P(None, None, ("dp", "seq")),
        P(None, ("dp", "seq"), None),
        P(None, ("dp", "seq"), None),
        P(None, None, ("dp", "seq")),
    )
    out_specs = (
        P("dp", "seq", None),
        P("dp", "seq", None),
        P(None, ("dp", "seq"), None),
        P(None, ("dp", "seq"), None),
        P(None, ("dp", "seq"), None),
        P(None, ("dp", "seq"), None),
        P(None, ("dp", "seq"), None),
        P(None, ("dp", "seq"), None),
        P(None, None, ("dp", "seq")),
        P(None, None, ("dp", "seq")),
        P(None, None, ("dp", "seq")),
    )
    return jax.shard_map(local, mesh=mesh, in_specs=in_specs, out_specs=out_specs, check_vma=False)
```

profile of v0, /device:TPU:1, one launch (start us, length us, event | category | flops | bytes accessed | tf_op | source)
XLA Modules:
  0.0 845.7 jit_solution(8866178216099717560)
XLA Ops:
  11.2 180.7 %all_gather.27 = bf16[2,12,512]{1,0,2:T(2,128)(2,1)S(1)} all-gather(bf16[2,12,4]{1,0,2:T(2,128)(2,1)S(1)} %copy.161), channel_id=1, replica_groups=mesh['dp'=32,'seq'=4] {'dp','seq'}, dimensions={2}, use_global_device_ids=true | all-gather | bytes 24768 | tf_op jit(solution)/shard_map/all_gather | solution.py:284
  193.6 5.2 all_gather.29
  198.9 34.3 %slice_reduce_fusion.1 = (f32[512]{0:T(512)}, f32[512]{0:T(512)}, f32[512]{0:T(512)}, f32[512]{0:T(512)}, f32[512]{0:T(512)}, /*index=5*/f32[512]{0:T(512)}, f32...) fusion(f32[2,12,512]{1,0,2:T(2,128)S(1)} %convert_element_type.312), kind=kLoop, calls=%fused_computation.145 | loop fusion | bytes 65536 | tf_op jit(solution)/shard_map/slice | solution.py:111
  233.2 9.9 %fusion.160 = (bf16[1,512,2048]{2,0,1:T(2,128)(2,1)S(1)}, bf16[1,512,2048]{2,0,1:T(2,128)(2,1)}) fusion(bf16[2,512,2048]{2,0,1:T(2,128)(2,1)} %all-gather.3.cloned.1.call-done), kind=kLoop, calls=%fused_computation.273 | loop fusion | bytes 8388608 | tf_op jit(solution)/shard_map/slice | solution.py:295
  245.8 8.3 all_gather.31
  254.3 8.8 %all_gather.28 = bf16[1,512,512]{2,1,0:T(8,128)(2,1)S(1)} all-gather(bf16[1,128,512]{2,1,0:T(8,128)(2,1)} %get-tuple-element.95), channel_id=1, replica_groups=mesh['dp'=32,'seq'=4] {'seq'}, dimensions={1}, use_global_device_ids=true | all-gather | bytes 655360 | tf_op jit(solution)/shard_map/all_gather | solution.py:66
  263.3 5.0 copy.162
  272.0 143.3 %all-gather.5.cloned.1.call-done = bf16[2,512,4096]{2,0,1:T(2,128)(2,1)} async-done(((bf16[2,4,4096]{2,0,1:T(2,128)(2,1)}), bf16[2,512,4096]{2,0,1:T(2,128)(2,1)}) %all-gather.5.cloned.1.call-update) | async-done | bytes 8388624 | tf_op jit(solution)/shard_map/all_gather | solution.py:283
  415.2 19.4 %fusion.159 = (bf16[1,512,4096]{2,0,1:T(2,128)(2,1)S(1)}, bf16[1,512,4096]{2,0,1:T(2,128)(2,1)S(1)}) fusion(bf16[2,512,4096]{2,0,1:T(2,128)(2,1)} %all-gather.5.cloned.1.call-done), kind=kLoop, calls=%fused_computation.272 | loop fusion | bytes 16777216 | tf_op jit(solution)/shard_map/slice | solution.py:296
  434.6 11.1 %copy_bitcast_fusion = (bf16[512,4096]{1,0:T(8,128)(2,1)}, bf16[512,4096]{1,0:T(8,128)(2,1)S(1)}) fusion(bf16[1,512,4096]{2,0,1:T(2,128)(2,1)S(1)} %get-tuple-element.89, bf16[1,512,4096]{2,0,1:T(2,128)(2,1)S(1)} %get-tuple-element.88), kind=kLoop, calls=%fused_computation.4 | loop fusion | bytes 16777216 | tf_op jit(solution)/shard_map/squeeze | solution.py:296
  445.7 3.7 multiply_convert_fusion.3
  452.5 7.7 all_gather.34
  460.4 8.9 %all_gather.33 = bf16[1,512,512]{2,1,0:T(8,128)(2,1)} all-gather(bf16[1,128,512]{2,1,0:T(8,128)(2,1)} %get-tuple-element.93), channel_id=1, replica_groups=mesh['dp'=32,'seq'=4] {'seq'}, dimensions={1}, use_global_device_ids=true | all-gather | bytes 655360 | tf_op jit(solution)/shard_map/all_gather | solution.py:66
  498.3 3.6 copy.122
  504.1 3.9 fusion.139
  516.3 7.7 pad_maximum_fusion.1
  525.2 7.3 reduce-scatter.17.cloned.1.call-done
  537.0 3.1 convert_reduce_fusion.1
  564.2 4.3 pad_maximum_fusion.3
  568.9 5.5 copy.116
  574.9 7.7 pad_maximum_fusion
  583.9 8.2 reduce-scatter.21.cloned.1.call-done
  604.8 67.3 %all-reduce.6 = (f32[512,12]{0,1:T(8,128)S(1)}, f32[512,12]{0,1:T(8,128)S(1)}) all-reduce(f32[512,12]{0,1:T(8,128)S(1)} %bitcast.295, f32[512,12]{0,1:T(8,128)S(1)} %bitcast.296), channel_id=11, replica_groups=mesh['dp'=32,'seq'=4] {'dp','seq'}, use_global_device_ids=true, to_apply=%region_49.50.clone | all-reduce | flops 12288 | bytes 98304
  676.1 155.0 %all-reduce.10.cloned.1.call-done = (f32[512,2048]{0,1:T(8,128)}, f32[512,2048]{0,1:T(8,128)}, f32[512,4096]{1,0:T(8,128)}, f32[512,4096]{1,0:T(8,128)}) async-done(((f32[512,2048]{0,1:T(8,128)}, f32[512,2048]{0,1:T(8,128)}, f32[512,4096]{1,0:T(8,128)}, f32[512,4096]{1,0:T(8,128)}), (f32[512,2048]{0,1:T(8,128)}, f32[512,2048]{0,1:T(8,128)}, f32[512,4096]{1,0:T(8,128)}, ...) | async-done | bytes 25165840
  (355 shorter events, 110.1 us)
Async XLA Ops:
  7.2 186.4 %copy-start.100 = (s32[1,128]{1,0:T(1,128)S(1)}, s32[1,128]{1,0:T(1,128)}, u32[]{:S(2)}) copy-start(s32[1,128]{1,0:T(1,128)} %param.14) | copy-start | bytes 1540
  7.2 226.0 %all-gather.3.cloned.1.call-start = ((), (), s32[]{:S(2)}) async-start(), calls=%async_computation.4 | async-start | bytes 4227072 | tf_op jit(solution)/shard_map/all_gather | solution.py:282
  8.8 406.5 %all-gather.5.cloned.1.call-start = ((), (), s32[]{:S(2)}) async-start(), calls=%async_computation.5 | async-start | bytes 8454144 | tf_op jit(solution)/shard_map/all_gather | solution.py:283
  10.5 513.5 %reduce-scatter.19.cloned.1.call-start = ((), (), s32[]{:S(2)}) async-start(), calls=%async_computation.7 | async-start | bytes 655360
  198.9 69.4 %copy-start.34 = (pred[128,512]{1,0:T(8,128)(4,1)}, pred[128,512]{1,0:T(8,128)(4,1)S(1)}, u32[]{:S(2)}) copy-start(pred[128,512]{1,0:T(8,128)(4,1)S(1)} %broadcast_compare_fusion) | copy-start | bytes 196612
  233.2 216.3 %copy-start.60 = (f32[512]{0:T(512)}, f32[512]{0:T(512)S(1)}, u32[]{:S(2)}) copy-start(f32[512]{0:T(512)S(1)} %get-tuple-element.51) | copy-start | bytes 6148
  233.2 216.3 %copy-start.74 = (f32[512]{0:T(512)}, f32[512]{0:T(512)S(1)}, u32[]{:S(2)}) copy-start(f32[512]{0:T(512)S(1)} %get-tuple-element.50) | copy-start | bytes 6148
  245.8 22.5 %copy-start.32 = (bf16[1,128,512]{1,2,0:T(8,128)(2,1)}, bf16[1,128,512]{1,2,0:T(8,128)(2,1)S(1)}, u32[]{:S(2)}) copy-start(bf16[1,128,512]{1,2,0:T(8,128)(2,1)S(1)} %copy.102) | copy-start | bytes 393220
  270.3 164.3 %copy-start.53 = (bf16[8,64,128]{2,1,0:T(8,128)(2,1)}, bf16[8,64,128]{2,1,0:T(8,128)(2,1)S(1)}, u32[]{:S(2)}) copy-start(bf16[8,64,128]{2,1,0:T(8,128)(2,1)S(1)} %convolution_convert_fusion.5) | copy-start | bytes 393220
  271.7 177.8 %copy-start.11 = (f32[1,128,512]{2,1,0:T(8,128)}, f32[1,128,512]{2,1,0:T(8,128)S(1)}, u32[]{:S(2)}) copy-start(f32[1,128,512]{2,1,0:T(8,128)S(1)} %get-tuple-element.102) | copy-start | bytes 786436
  271.7 177.8 %copy-start.81 = (f32[128]{0:T(128)}, f32[128]{0:T(128)S(1)}, u32[]{:S(2)}) copy-start(f32[128]{0:T(128)S(1)} %broadcast_multiply_fusion.3) | copy-start | bytes 1540
  271.9 162.7 %copy-start.101 = (f32[128]{0:T(128)}, f32[128]{0:T(128)S(1)}, u32[]{:S(2)}) copy-start(f32[128]{0:T(128)S(1)} %multiply_reduce_fusion.11) | copy-start | bytes 1540
  271.9 177.6 %copy-start.91 = (f32[128]{0:T(128)}, f32[128]{0:T(128)S(1)}, u32[]{:S(2)}) copy-start(f32[128]{0:T(128)S(1)} %fusion.122) | copy-start | bytes 1540
  494.5 38.0 %reduce-scatter.17.cloned.1.call-start = ((), (), s32[]{:S(2)}) async-start(), calls=%async_computation.6 | async-start | bytes 655360
  510.9 71.8 %reduce-scatter.23.cloned.1.call-start = ((), (), s32[]{:S(2)}) async-start(), calls=%async_computation.9 | async-start | bytes 655360
  516.3 17.5 %copy-start.68 = (f32[128]{0:T(128)S(1)}, f32[128]{0:T(128)}, u32[]{:S(2)}) copy-start(f32[128]{0:T(128)} %copy-done.66) | copy-start | bytes 1540
  516.3 17.5 %copy-start.72 = (f32[128]{0:T(128)S(1)}, f32[128]{0:T(128)}, u32[]{:S(2)}) copy-start(f32[128]{0:T(128)} %copy-done.70) | copy-start | bytes 1540
  516.3 17.5 %copy-start.85 = (f32[128]{0:T(128)S(1)}, f32[128]{0:T(128)}, u32[]{:S(2)}) copy-start(f32[128]{0:T(128)} %copy-done.84) | copy-start | bytes 1540
  551.5 40.6 %reduce-scatter.21.cloned.1.call-start = ((), (), s32[]{:S(2)}) async-start(), calls=%async_computation.8 | async-start | bytes 655360
  563.8 267.2 %all-reduce.10.cloned.1.call-start = ((), (), s32[]{:S(2)}) async-start(), calls=%async_computation.10 | async-start | bytes 50331648
  574.9 18.4 %copy-start.50 = (bf16[8,64,128]{2,1,0:T(8,128)(2,1)}, bf16[8,64,128]{2,1,0:T(8,128)(2,1)S(1)}, u32[]{:S(2)}) copy-start(bf16[8,64,128]{2,1,0:T(8,128)(2,1)S(1)} %get-tuple-element.125) | copy-start | bytes 393220
  574.9 18.4 %copy-start.31 = (bf16[1,128,512]{2,1,0:T(8,128)(2,1)S(1)}, bf16[1,128,512]{2,1,0:T(8,128)(2,1)}, u32[]{:S(2)}) copy-start(bf16[1,128,512]{2,1,0:T(8,128)(2,1)} %param.12) | copy-start | bytes 393220
  596.3 77.5 %copy-start.3 = (bf16[1,512,2048]{2,1,0:T(8,128)(2,1)S(1)}, bf16[1,512,2048]{2,1,0:T(8,128)(2,1)}, u32[]{:S(2)}) copy-start(bf16[1,512,2048]{2,1,0:T(8,128)(2,1)} %copy-done.2) | copy-start | bytes 6291460
  596.3 77.5 %copy-start.43 = (bf16[1,128,512]{1,2,0:T(8,128)(2,1)S(1)}, bf16[1,128,512]{1,2,0:T(8,128)(2,1)}, u32[]{:S(2)}) copy-start(bf16[1,128,512]{1,2,0:T(8,128)(2,1)} %copy-done.42) | copy-start | bytes 393220
  (88 other events, 331.8 us)
Sparse Core Ops, SparseCore 0:
  10.3 200.8 all-gather.2
  213.5 201.7 all-gather.4
  494.6 16.4 reduce-scatter.18
  513.4 19.0 reduce-scatter.16
  551.6 18.9 reduce-scatter.22
  572.8 19.2 reduce-scatter.20
  598.2 232.8 all-reduce.9
where the time goes:
time: 850 us; the launch traced here: 846 us
  waiting for transfers between devices  314 us (37%)
  blocking collectives  287 us (34%)
  local copies, waits for them, and re-layouts  128 us (15%)
  matrix products  60.9 us (7%)
  other arithmetic  39.2 us (5%)
  between operations  15.8 us (2%)
    all_gather x1, blocking collectives, local(): lax.all_gather(vectors.astype(jnp.bfloat16), ('dp', 'seq'), axis=2, tiled...  181 us
    unnamed x12, waiting for transfers between devices  171 us
    all_gather x1, waiting for transfers between devices, local(): lax.all_gather(w_mlp.astype(jnp.bfloat16), ('dp', 'seq'), axis=1, tiled=T...  143 us
    unnamed x1, blocking collectives  67.3 us
    slice x1, local copies, waits for them, and re-layouts, forward_layer(): vec_layer[6 + inner_rows]  34.3 us
    unnamed x233, local copies, waits for them, and re-layouts  33.7 us
    slice x1, local copies, waits for them, and re-layouts, local(): gathered_mlp[layer_index]  19.4 us
    all_gather x2, blocking collectives, forward_layer(): lax.all_gather(value_local, 'seq', axis=1, tiled=True)  17.7 us
  transfers between devices with their start and end apart: 7, of which 4 were waited for; matrix products, arithmetic and copies ran while one was open for 16% of the time, Pallas kernels for 0%

commit v1 on v0

v1 whole, which is shorter than its diff:
```python
import math

import jax
import jax.numpy as jnp
from jax import lax
from jax.experimental import pallas as pl
from jax.experimental.pallas import tpu as pltpu
from jax.sharding import PartitionSpec as P

STEP = 10
NORM_EPSILON = 1e-06
ADAM_EPSILON = 1e-06
BETA_FIRST = 0.9
BETA_SECOND = 0.999
LEARN_RATE = 0.03
VECTOR_RATE = 0.2
WEIGHT_DECAY = 0.01
MASKED_SCORE = -1e30
VMEM_BYTES = 62 * 2**20
MESH = pl.DeviceIdType.MESH
BF = jnp.bfloat16
F32 = jnp.float32
THIRDS = (((0, 128), (128, 256), (256, 512)), ((0, 384), (384, 768), (768, 1024)))
WIDTHS = (512, 1024)
ORDERS = (("x", "y", "z"), ("y", "z", "x"), ("z", "x", "y"))


class Place:
    def __init__(self):
        self.dp = lax.axis_index("dp")
        self.seq = lax.axis_index("seq")
        self.core = self.seq % 2
        self.at = {
            "x": ((self.dp // 4) % 2) * 2 + self.seq // 2,
            "y": self.dp // 8,
            "z": self.dp % 4,
        }

    def device(self, at, core):
        return {
            "dp": (at["y"] * 2 + at["x"] // 2) * 4 + at["z"],
            "seq": (at["x"] % 2) * 2 + core,
        }

    def along(self, axis, step):
        at = dict(self.at)
        at[axis] = (at[axis] + step) % 4
        return at[axis], self.device(at, self.core)

    def other_core(self):
        return self.device(self.at, 1 - self.core)

    def in_group(self, step):
        peer = (self.seq + step) % 4
        return peer, {"dp": self.dp, "seq": peer}


def region(buf, layer, at, core, columns):
    whole = slice(None)
    if "x" in at:
        x_hi, x_lo = at["x"] // 2, at["x"] % 2
    else:
        x_hi, x_lo = whole, whole
    cols = pl.ds(columns[0], columns[1] - columns[0])
    return buf.at[layer, x_lo, core, at.get("y", whole), x_hi, at.get("z", whole), whole, cols]


def greet(place):
    barrier = pltpu.get_barrier_semaphore()
    peers = [place.other_core()]
    for axis in ("x", "y", "z"):
        for step in (1, 2, 3):
            peers.append(place.along(axis, step)[1])
    far = {"dp": place.dp, "seq": (1 - place.seq // 2) * 2 + (1 - place.core)}
    peers.append(far)
    for peer in peers:
        pl.semaphore_signal(barrier, inc=1, device_id=peer, device_id_type=MESH)
    pl.semaphore_wait(barrier, len(peers))


def remote(src, dst, send, recv, device):
    return pltpu.make_async_remote_copy(
        src_ref=src, dst_ref=dst, send_sem=send, recv_sem=recv, device_id=device, device_id_type=MESH
    )


def share_vectors(place, vsum, vgot, v_send, v_recv):
    for rnd, axis in enumerate(("core", "x", "y", "z")):
        steps = (1,) if axis == "core" else (1, 2, 3)
        copies = []
        for step in steps:
            device = place.other_core() if axis == "core" else place.along(axis, step)[1]
            copy = remote(vsum, vgot.at[rnd, step - 1], v_send.at[rnd, step - 1], v_recv.at[rnd, step - 1], device)
            copy.start()
            copies.append(copy)
        for copy in copies:
            copy.wait()
        total = vsum[...]
        for step in steps:
            total = total + vgot[rnd, step - 1]
        vsum[...] = total


def dims_of(axes):
    out = ()
    if "x" in axes:
        out += (2,)
    if "y" in axes:
        out += (4,)
    if "x" in axes:
        out += (2,)
    if "z" in axes:
        out += (4,)
    return out


def each_block(dims, body):
    count = 1
    for size in dims:
        count *= size

    def one(i, carry):
        index = ()
        rest = i
        for size in reversed(dims):
            index = (rest % size,) + index
            rest = rest // size
        body(index)
        return carry

    if count == 1:
        body(tuple(0 for _ in dims))
    else:
        lax.fori_loop(0, count, one, 0)


NT = (((1,), (1,)), ((), ()))
NN = (((1,), (0,)), ((), ()))
TN = (((0,), (0,)), ((), ()))
CHUNKS = ((0, 0), (0, 1), (1, 0), (1, 1))
PIECES = (16, 1536)
SCALE = 0.125


def mm(left, right, dims=NN):
    return lax.dot_general(left, right, dims, preferred_element_type=F32)


def column_sum(values):
    return jnp.sum(values, axis=0, keepdims=True)


def normalize(summed):
    center = summed - jnp.mean(summed, axis=-1, keepdims=True)
    spread = jnp.mean(center * center, axis=-1, keepdims=True)
    inverse = lax.rsqrt(spread + NORM_EPSILON)
    return center * inverse, inverse


def normalize_back(grad, hat, inverse):
    mean = jnp.mean(grad, axis=-1, keepdims=True)
    along = jnp.mean(grad * hat, axis=-1, keepdims=True)
    return inverse * (grad - mean - hat * along)


class Gather:
    def __init__(self, place, bufs, send, recv, swap_send, swap_recv):
        self.place, self.bufs = place, bufs
        self.send, self.recv, self.swap_send, self.swap_recv = send, recv, swap_send, swap_recv

    def copies(self, l, arr, phase, coming):
        place = self.place
        out = []
        for j, order in enumerate(ORDERS):
            axis = order[phase]
            here = {a: place.at[a] for a in order[phase:]}
            for step in (1, 2, 3):
                _, device = place.along(axis, step)
                spot = dict(here)
                if coming:
                    spot[axis] = (place.at[axis] - step) % 4
                ref = region(self.bufs[arr], l, spot, place.core, THIRDS[arr][j])
                sems = (self.send.at[l, arr, phase, j, step - 1], self.recv.at[l, arr, phase, j, step - 1])
                out.append(remote(ref, ref, *sems, device))
        return out

    def start(self, l, arr, phase):
        for copy in self.copies(l, arr, phase, False):
            copy.start()

    def arrive(self, l, arr, phase):
        for copy in self.copies(l, arr, phase, True):
            copy.wait_recv()

    def swap(self, l, arr):
        mine = self.bufs[arr].at[l, :, self.place.core]
        return remote(mine, mine, self.swap_send.at[l, arr], self.swap_recv.at[l, arr], self.place.other_core())

    def swap_start(self, l, arr):
        self.arrive(l, arr, 2)
        self.swap(l, arr).start()

    def swap_arrive(self, l, arr):
        theirs = self.bufs[arr].at[l, :, 1 - self.place.core]
        remote(
            theirs, theirs, self.swap_send.at[l, arr], self.swap_recv.at[l, arr], self.place.other_core()
        ).wait_recv()

    def finish(self):
        for chunk in CHUNKS:
            for phase in range(3):
                for copy in self.copies(*chunk, phase, False):
                    copy.wait_send()
            self.swap(*chunk).wait_send()


class Scatter:
    def __init__(self, place, bufs, landed, slots, total, swap_send, swap_recv, send, recv):
        self.place, self.bufs, self.landed, self.slots, self.total = place, bufs, landed, slots, total
        self.swap_send, self.swap_recv, self.send, self.recv = swap_send, swap_recv, send, recv

    def slot(self, phase, arr, j):
        return self.slots[(phase * 2 + arr) * 3 + j]

    def swap(self, l, arr):
        return remote(
            self.bufs[arr].at[l, :, 1 - self.place.core],
            self.landed[arr].at[l],
            self.swap_send.at[l, arr],
            self.swap_recv.at[l, arr],
            self.place.other_core(),
        )

    def copies(self, l, arr, phase):
        place = self.place
        out = []
        for j, order in enumerate(ORDERS):
            rev = order[::-1]
            for step in (1, 2, 3):
                there = {a: place.at[a] for a in rev[:phase]}
                there[rev[phase]], device = place.along(rev[phase], step)
                src = region(self.bufs[arr], l, there, place.core, THIRDS[arr][j])
                dst = self.slot(phase, arr, j).at[l, step - 1]
                sems = (self.send.at[l, arr, phase, j, step - 1], self.recv.at[l, arr, phase, j, step - 1])
                out.append(remote(src, dst, *sems, device))
        return out

    def add_up(self, l, arr, phase):
        for j, order in enumerate(ORDERS):
            rev = order[::-1]
            here = {a: self.place.at[a] for a in rev[: phase + 1]}
            own = region(self.bufs[arr], l, here, self.place.core, THIRDS[arr][j])
            came = self.slot(phase, arr, j)

            def body(index, own=own, came=came, j=j):
                total = own[index].astype(F32)
                for k in range(3):
                    total = total + came[(l, k) + index].astype(F32)
                if phase < 2:
                    own[index] = total.astype(BF)
                else:
                    low, high = THIRDS[arr][j]
                    self.total[l, :, 512 * arr + low : 512 * arr + high] = total

            each_block(dims_of(rev[phase + 1 :]), body)

    def begin(self, l, arr):
        self.swap(l, arr).start()

    def step(self, l, arr, stage):
        if stage == 0:
            self.swap(l, arr).wait_recv()

            def body(index):
                own = self.bufs[arr].at[(l, index[0], self.place.core) + index[1:]]
                own[...] = (own[...].astype(F32) + self.landed[arr][(l,) + index].astype(F32)).astype(BF)

            each_block((2, 4, 2, 4), body)
        else:
            for copy in self.copies(l, arr, stage - 1):
                copy.wait_recv()
            self.add_up(l, arr, stage - 1)
        if stage < 3:
            for copy in self.copies(l, arr, stage):
                copy.start()

    def finish(self):
        for chunk in CHUNKS:
            self.swap(*chunk).wait_send()
            for phase in range(3):
                for copy in self.copies(*chunk, phase):
                    copy.wait_send()


def train_kernel(*refs):
    names = NAMES
    r = dict(zip(names, refs[: len(names)]))
    slots = refs[len(names) :]
    place = Place()
    seq = place.seq
    wa, wm, ga, gm, vec, vgrad = r["wa"], r["wm"], r["ga"], r["gm"], r["vec"], r["vgrad"]
    s0, r0, stage, kv = r["s0"], r["r0"], r["stage"], r["kv"]
    unsent = []

    for q in range(4):
        for l in range(2):
            s0[q, l, :, 0:512] = r["w_attn"][l, :, 512 * q : 512 * q + 512]
            s0[q, l, :, 512:1536] = r["w_mlp"][l, :, 1024 * q : 1024 * q + 1024]
    vec[...] = r["table"][...]
    r["docs"][seq] = r["seg_row"][...]
    greet(place)

    def to_group(src, dst, send, recv):
        out = []
        for step in (1, 2, 3):
            peer, device = place.in_group(step)
            copy = remote(src(peer, step), dst(step), send.at[step], recv.at[step], device)
            copy.start()
            out.append(copy)
            unsent.append(copy)
        return out

    pieces = to_group(lambda peer, step: s0.at[peer], lambda step: r0.at[seq], r["a2a_send"].at[0], r["a2a_recv"].at[0])
    docs = to_group(lambda peer, step: r["docs"].at[seq], lambda step: r["docs"].at[seq], r["doc_send"], r["doc_recv"])
    r0[seq] = s0[seq]
    for copy in pieces:
        copy.wait_recv()
    for src in range(4):
        for l in range(2):
            stage[l, 4 * src : 4 * src + 4, :] = r0[src, l]
    at = place.at
    for l, arr in CHUNKS:
        block = stage[l, :, 512 * arr : 512 * arr + WIDTHS[arr]].astype(BF)
        (wa, wm)[arr][l, at["x"] % 2, place.core, at["y"], at["x"] // 2, at["z"]] = block
    gather = Gather(place, (wa, wm), r["ag_send"], r["ag_recv"], r["sw_send"], r["sw_recv"])
    for phase in range(3):
        for chunk in CHUNKS:
            if phase > 0:
                gather.arrive(*chunk, phase - 1)
            gather.start(*chunk, phase)
    share_vectors(place, vec, r["vgot"].at[0], r["v_send"].at[0], r["v_recv"].at[0])
    for copy in docs:
        copy.wait_recv()
    seg_row = jnp.concatenate([r["docs"][i] for i in range(4)], axis=1)
    r["bias"][...] = jnp.where(r["seg_col"][...] == seg_row, 0.0, MASKED_SCORE)
    gather.swap_start(0, 0)
    gather.swap_arrive(0, 0)

    def weight(l, arr, q, low=0, high=None):
        return (wa, wm)[arr][l, q // 2, q % 2, :, :, :, :, low : WIDTHS[arr] if high is None else high].reshape(
            512, (WIDTHS[arr] if high is None else high) - low
        )

    def put_grad(l, arr, q, low, value):
        width = value.shape[1]
        (ga, gm)[arr][l, q // 2, q % 2, :, :, :, :, low : low + width] = value.astype(BF).reshape(4, 2, 4, 16, width)

    def row(l, k):
        return vec[12 * l + k : 12 * l + k + 1, :]

    def put_row(l, k, value):
        vgrad[12 * l + k : 12 * l + k + 1, :] = value

    lanes = lax.broadcasted_iota(jnp.int32, (1, 128), 1)
    first = (lanes < 64).astype(F32)
    second = 1.0 - first
    first_low, second_low = first.astype(BF), second.astype(BF)

    def both(pair):
        return jnp.concatenate([pair * first_low, pair * second_low], axis=0)

    def joined(stacked):
        return stacked[:128] * first + stacked[128:] * second

    def group_rows(ref, l, which, low):
        return ref[l, :, which, :, low : low + 128].reshape(512, 128)

    hidden = r["tokens"][...].astype(F32)
    for l in range(2):
        if l == 1:
            gather.swap_arrive(1, 0)
        low_in = hidden.astype(BF)
        r["x"][l] = low_in
        kv[l, seq, 0] = mm(low_in, weight(l, 0, 1)).astype(BF)
        kv[l, seq, 1] = (mm(low_in, weight(l, 0, 2)) + row(l, 1)).astype(BF)
        moved = to_group(
            lambda peer, step: kv.at[l, seq], lambda step: kv.at[l, seq], r["kv_send"].at[l], r["kv_recv"].at[l]
        )
        r["q"][l] = (mm(low_in, weight(l, 0, 0)) + row(l, 0)).astype(BF)
        if l == 0:
            gather.swap_start(0, 1)
        for copy in moved:
            copy.wait_recv()
        for pair in range(4):
            low = 128 * pair
            keys, values = group_rows(kv, l, 0, low), group_rows(kv, l, 1, low)
            scores = mm(both(r["q"][l, :, low : low + 128]), keys, NT) * SCALE
            bias = r["bias"][...]
            scores = scores + jnp.concatenate([bias, bias], axis=0)
            powers = jnp.exp(scores - jnp.max(scores, axis=-1, keepdims=True))
            probs = (powers * (1.0 / jnp.sum(powers, axis=-1, keepdims=True))).astype(BF)
            r["probs"][l, pair] = probs
            r["o"][l, :, low : low + 128] = joined(mm(probs, values)).astype(BF)
        if l == 0:
            gather.swap_arrive(0, 1)
            gather.swap_start(1, 0)
        else:
            gather.swap_arrive(1, 1)
        hat, inverse = normalize(hidden + mm(r["o"][l], weight(l, 0, 3)) + row(l, 2))
        r["hat1"][l] = hat
        r["inv1"][l] = inverse
        normed = hat * row(l, 3) + row(l, 4)
        low_normed = normed.astype(BF)
        r["n1"][l] = low_normed
        back = jnp.zeros((128, 512), F32)
        for i in range(4):
            low = 512 * (i % 2)
            pre = mm(low_normed, weight(l, 1, i // 2, low, low + 512)) + row(l, 5 + i)
            normal = 0.5 + 0.5 * lax.erf(pre * (0.5**0.5))
            act = (pre * normal).astype(BF)
            r["act"][l, :, 512 * i : 512 * i + 512] = act
            slope = normal + pre * (jnp.exp(pre * pre * -0.5) * (1.0 / (2.0 * math.pi) ** 0.5))
            r["slope"][l, :, 512 * i : 512 * i + 512] = slope.astype(BF)
            back = back + mm(act, weight(l, 1, 2 + i // 2, low, low + 512), NT)
            if l == 0 and i == 1:
                gather.swap_start(1, 1)
        hat, inverse = normalize(normed + back + row(l, 9))
        r["hat2"][l] = hat
        r["inv2"][l] = inverse
        hidden = hat * row(l, 10) + row(l, 11)
    r["block_out"][...] = hidden.astype(BF)

    scatter = Scatter(
        place, (ga, gm), (r["r0a"], r["r0m"]), slots, r["total"], r["gs_send"], r["gs_recv"], r["rs_send"], r["rs_recv"]
    )
    grad = r["cotangent"][...].astype(F32)
    for l in (1, 0):
        hat = r["hat2"][l]
        put_row(l, 10, column_sum(grad * hat))
        put_row(l, 11, column_sum(grad))
        grad_second = normalize_back(grad * row(l, 10), hat, r["inv2"][l])
        put_row(l, 9, column_sum(grad_second))
        low_second = grad_second.astype(BF)
        grad_normed = grad_second
        for i in range(4):
            low = 512 * (i % 2)
            span = slice(512 * i, 512 * i + 512)
            grad_act = mm(low_second, weight(l, 1, 2 + i // 2, low, low + 512))
            grad_pre = (grad_act * r["slope"][l, :, span].astype(F32)).astype(BF)
            put_row(l, 5 + i, column_sum(grad_pre.astype(F32)))
            put_grad(l, 1, 2 + i // 2, low, mm(low_second, r["act"][l, :, span], TN))
            put_grad(l, 1, i // 2, low, mm(r["n1"][l], grad_pre, TN))
            grad_normed = grad_normed + mm(grad_pre, weight(l, 1, i // 2, low, low + 512), NT)
            if l == 0 and i == 0:
                scatter.step(1, 1, 1)
                scatter.step(1, 0, 0)
            if l == 0 and i == 2:
                scatter.step(1, 1, 2)
                scatter.step(1, 0, 1)
        scatter.begin(l, 1)
        hat = r["hat1"][l]
        put_row(l, 3, column_sum(grad_normed * hat))
        put_row(l, 4, column_sum(grad_normed))
        grad_first = normalize_back(grad_normed * row(l, 3), hat, r["inv1"][l])
        put_row(l, 2, column_sum(grad_first))
        low_first = grad_first.astype(BF)
        put_grad(l, 0, 3, 0, mm(r["o"][l], low_first, TN))
        grad_mixed = mm(low_first, weight(l, 0, 3), NT).astype(BF)
        dkv_out, dkv_in = r["dkv_out"], r["dkv_in"]
        for pair in range(4):
            low = 128 * pair
            keys, values = group_rows(kv, l, 0, low), group_rows(kv, l, 1, low)
            grad_pair = both(grad_mixed[:, low : low + 128])
            probs = r["probs"][l, pair]
            grad_probs = mm(grad_pair, values, NT)
            dkv_out[l, :, 1, :, low : low + 128] = mm(probs, grad_pair, TN).astype(BF).reshape(4, 128, 128)
            wide = probs.astype(F32)
            row_dot = jnp.sum(grad_probs * wide, axis=-1, keepdims=True)
            grad_scores = (wide * (grad_probs - row_dot)).astype(BF)
            r["dq"][:, low : low + 128] = (joined(mm(grad_scores, keys)) * SCALE).astype(BF)
            grad_keys = mm(grad_scores, both(r["q"][l, :, low : low + 128]), TN) * SCALE
            dkv_out[l, :, 0, :, low : low + 128] = grad_keys.astype(BF).reshape(4, 128, 128)
        moved = to_group(
            lambda peer, step: dkv_out.at[l, peer],
            lambda step: dkv_in.at[l, step - 1],
            r["dkv_send"].at[l],
            r["dkv_recv"].at[l],
        )
        low_in = r["x"][l]
        grad_queries = r["dq"][...]
        put_row(l, 0, column_sum(grad_queries.astype(F32)))
        put_grad(l, 0, 0, 0, mm(low_in, grad_queries, TN))
        grad = grad_first + mm(grad_queries, weight(l, 0, 0), NT)
        if l == 0:
            scatter.step(1, 1, 3)
            scatter.step(1, 0, 2)
        scatter.step(l, 1, 0)
        for copy in moved:
            copy.wait_recv()
        for which in range(2):
            total = dkv_out[l, seq, which].astype(F32)
            for k in range(3):
                total = total + dkv_in[l, k, which].astype(F32)
            low_total = total.astype(BF)
            if which == 1:
                put_row(l, 1, column_sum(low_total.astype(F32)))
            put_grad(l, 0, 1 + which, 0, mm(low_in, low_total, TN))
            grad = grad + mm(low_total, weight(l, 0, 1 + which), NT)
        scatter.begin(l, 0)
    r["input_grad"][...] = grad
    scatter.step(1, 0, 3)
    scatter.step(0, 1, 1)
    scatter.step(0, 0, 0)
    share_vectors(place, vgrad, r["vgot"].at[1], r["v_send"].at[1], r["v_recv"].at[1])
    scatter.step(0, 1, 2)
    scatter.step(0, 0, 1)
    scatter.step(0, 1, 3)
    scatter.step(0, 0, 2)
    scatter.step(0, 0, 3)
    s4, fin, total = r["s4"], r["fin"], r["total"]
    for dst in range(4):
        for l in range(2):
            s4[dst, l] = total[l, 4 * dst : 4 * dst + 4, :]
    moved = to_group(lambda peer, step: s4.at[peer], lambda step: fin.at[seq], r["a2a_send"].at[1], r["a2a_recv"].at[1])
    fin[seq] = s4[seq]
    gather.finish()
    scatter.finish()
    for copy in moved:
        copy.wait_recv()
    for copy in unsent:
        copy.wait_send()


INPUTS = ("tokens", "cotangent", "seg_row", "seg_col", "w_attn", "w_mlp", "table")
OUTPUTS = {
    "block_out": ((128, 512), BF),
    "input_grad": ((128, 512), F32),
    "fin": ((4, 2, 4, 1536), F32),
    "vgrad": ((24, 512), F32),
}
DIMS = (2, 2, 2, 4, 2, 4, 16)
HALF = (2, 2, 4, 2, 4, 16)
SCRATCH = {
    "wa": (DIMS + (512,), BF),
    "wm": (DIMS + (1024,), BF),
    "ga": (DIMS + (512,), BF),
    "gm": (DIMS + (1024,), BF),
    "r0a": (HALF + (512,), BF),
    "r0m": (HALF + (1024,), BF),
    "vec": ((24, 512), F32),
    "s0": ((4, 2, 4, 1536), F32),
    "r0": ((4, 2, 4, 1536), F32),
    "s4": ((4, 2, 4, 1536), F32),
    "stage": ((2, 16, 1536), F32),
    "total": ((2, 16, 1536), F32),
    "vgot": ((2, 4, 3, 24, 512), F32),
    "docs": ((4, 1, 128), jnp.int32),
    "bias": ((128, 512), F32),
    "x": ((2, 128, 512), BF),
    "q": ((2, 128, 512), BF),
    "kv": ((2, 4, 2, 128, 512), BF),
    "probs": ((2, 4, 256, 512), BF),
    "o": ((2, 128, 512), BF),
    "hat1": ((2, 128, 512), F32),
    "inv1": ((2, 128, 1), F32),
    "n1": ((2, 128, 512), BF),
    "act": ((2, 128, 2048), BF),
    "slope": ((2, 128, 2048), BF),
    "hat2": ((2, 128, 512), F32),
    "inv2": ((2, 128, 1), F32),
    "dq": ((128, 512), BF),
    "dkv_out": ((2, 4, 2, 128, 512), BF),
    "dkv_in": ((2, 3, 2, 128, 512), BF),
}
SEMS = {
    "a2a": (2, 4),
    "doc": (4,),
    "ag": (2, 2, 3, 3, 3),
    "sw": (2, 2),
    "gs": (2, 2),
    "rs": (2, 2, 3, 3, 3),
    "kv": (2, 4),
    "dkv": (2, 4),
    "v": (2, 4, 3),
}
NAMES = INPUTS + tuple(OUTPUTS) + tuple(SCRATCH) + tuple(f"{n}_{d}" for n in SEMS for d in ("send", "recv"))


def train(*args):
    slots = []
    for phase in range(3):
        for arr in range(2):
            for j in range(3):
                low, high = THIRDS[arr][j]
                rest = dims_of(ORDERS[j][::-1][phase + 1 :])
                slots.append(pltpu.VMEM((2, 3) + rest + (16, high - low), BF))
    scratch = [pltpu.VMEM(*spec) for spec in SCRATCH.values()]
    for shape in SEMS.values():
        scratch += [pltpu.SemaphoreType.DMA(shape)] * 2
    return pl.pallas_call(
        train_kernel,
        out_shape=tuple(jax.ShapeDtypeStruct(*spec) for spec in OUTPUTS.values()),
        in_specs=[pl.BlockSpec(memory_space=pltpu.VMEM)] * len(INPUTS),
        out_specs=[pl.BlockSpec(memory_space=pltpu.VMEM)] * len(OUTPUTS),
        scratch_shapes=scratch + slots,
        compiler_params=pltpu.CompilerParams(
            collective_id=0, has_side_effects=True, vmem_limit_bytes=VMEM_BYTES
        ),
        name="train",
    )(*args)


def adam_update(weight, grad, first, second, rate, decay):
    first_new = BETA_FIRST * first + (1.0 - BETA_FIRST) * grad
    second_new = BETA_SECOND * second + (1.0 - BETA_SECOND) * grad * grad
    first_fix = 1.0 - BETA_FIRST**STEP
    second_fix = 1.0 - BETA_SECOND**STEP
    weight_new = weight - rate * (
        first_new / first_fix / (jnp.sqrt(second_new / second_fix) + ADAM_EPSILON) + decay * weight
    )
    return (first_new, second_new, weight_new)


def local(
    tokens, cotangent, segments, w_attn, w_mlp, vectors, m_attn, m_mlp, m_vec, v_attn, v_mlp, v_vec
):
    place = lax.axis_index("dp") * 4 + lax.axis_index("seq")
    table = lax.dynamic_update_slice(
        jnp.zeros((24, 512), F32),
        vectors.astype(BF).astype(F32).reshape(24, 4),
        (0, 4 * place),
    )
    block_out, input_grad, fin, vec_total = train(
        tokens[0], cotangent[0], segments, segments.reshape(128, 1), w_attn, w_mlp, table
    )
    grad_attn = fin[..., :512].transpose(1, 2, 0, 3).reshape(2, 4, 2048)
    grad_mlp = fin[..., 512:].transpose(1, 2, 0, 3).reshape(2, 4, 4096)
    grad_vec = lax.dynamic_slice(vec_total, (0, 4 * place), (24, 4)).reshape(2, 12, 4)
    return (
        block_out[None],
        input_grad[None],
        *adam_update(w_attn, grad_attn, m_attn, v_attn, LEARN_RATE, WEIGHT_DECAY),
        *adam_update(w_mlp, grad_mlp, m_mlp, v_mlp, LEARN_RATE, WEIGHT_DECAY),
        *adam_update(vectors, grad_vec, m_vec, v_vec, VECTOR_RATE, 0.0),
    )


def solution(mesh):
    in_specs = (
        P("dp", "seq", None),
        P("dp", "seq", None),
        P("dp", "seq"),
        P(None, ("dp", "seq"), None),
        P(None, ("dp", "seq"), None),
        P(None, None, ("dp", "seq")),
        P(None, ("dp", "seq"), None),
        P(None, ("dp", "seq"), None),
        P(None, None, ("dp", "seq")),
        P(None, ("dp", "seq"), None),
        P(None, ("dp", "seq"), None),
        P(None, None, ("dp", "seq")),
    )
    out_specs = (
        P("dp", "seq", None),
        P("dp", "seq", None),
        P(None, ("dp", "seq"), None),
        P(None, ("dp", "seq"), None),
        P(None, ("dp", "seq"), None),
        P(None, ("dp", "seq"), None),
        P(None, ("dp", "seq"), None),
        P(None, ("dp", "seq"), None),
        P(None, None, ("dp", "seq")),
        P(None, None, ("dp", "seq")),
        P(None, None, ("dp", "seq")),
    )
    return jax.shard_map(local, mesh=mesh, in_specs=in_specs, out_specs=out_specs, check_vma=False)
```

time: 850 us -> 199 us (0.23)
  waiting for transfers between devices: 314 us -> 0 us
  blocking collectives: 287 us -> 0 us
  Pallas kernels: 0 us -> 189 us
  local copies, waits for them, and re-layouts: 128 us -> 7.02 us
  matrix products: 60.9 us -> 0 us
  other arithmetic: 39.2 us -> 2.31 us
  between operations: 15.8 us -> 0.74 us
    all_gather x6 -> x0, blocking collectives: 220 us -> none  [the longest x1 181 us: local(): lax.all_gather(vectors.astype(jnp.bfloat16), ('dp', 'seq'), axis=2, tiled...]
    pallas_call x0 -> x1, Pallas kernels: none -> 189 us  [train(): pl.pallas_call(train_kernel, out_shape=tuple((jax.ShapeDtypeStruct(*spec)...]
    unnamed x12 -> x0, waiting for transfers between devices: 171 us -> none
    all_gather x2 -> x0, waiting for transfers between devices: 143 us -> none  [the longest x1 143 us: local(): lax.all_gather(w_mlp.astype(jnp.bfloat16), ('dp', 'seq'), axis=1, tiled=T...]
    unnamed x1 -> x0, blocking collectives: 67.3 us -> none
    slice x8 -> x0, local copies, waits for them, and re-layouts: 64.4 us -> none  [the longest x1 34.3 us: forward_layer(): vec_layer[6 + inner_rows]]
    dot_general x36 -> x0, matrix products: 60.9 us -> none  [the longest x2 6.67 us: backward_layer(): jnp.einsum('std,stf->df', grad_back_low, activ_low, preferred_element_typ...]
    unnamed x233 -> x32, local copies, waits for them, and re-layouts: 33.7 us -> 4.66 us
  transfers between devices with their start and end apart: 7 -> 0, of which waited for: 4 -> 0; matrix products, arithmetic and copies ran while one was open for 16% -> 0% of each run, Pallas kernels for 0% -> 0%
where the time goes in v1:
time: 199 us
  Pallas kernels  189 us (95%)
  local copies, waits for them, and re-layouts  7.02 us (4%)
  other arithmetic  2.31 us (1%)
    pallas_call x1, Pallas kernels, train(): pl.pallas_call(train_kernel, out_shape=tuple((jax.ShapeDtypeStruct(*spec)...  189 us
    unnamed x32, local copies, waits for them, and re-layouts  4.66 us

profile of v1, /device:TPU:1, one launch (start us, length us, event | category | flops | bytes accessed | tf_op | source)
XLA Modules:
  0.0 198.9 jit_solution(12999288218099683529)
XLA Ops:
  0.7 0.7 copy-done.10
  1.3 0.1 reshape.47
  1.4 0.1 copy.48
  1.5 0.4 dynamic_update_slice.3.refs_6_
  2.0 0.2 copy-done.13
  2.2 0.7 copy.49.refs_3_
  2.9 188.8 %train.1 = (bf16[128,512]{1,0:T(8,128)(2,1)}, f32[128,512]{1,0:T(8,128)}, f32[4,2,4,1536]{3,2,1,0:T(4,128)}, f32[24,512]{1,0:T(8,128)}) custom-call(bf16[128,512]{1,0:T(8,128)(2,1)} %bitcast.21, bf16[128,512]{1,0:T(8,128)(2,1)} %bitcast.22, s32[1,128]{1,0:T(1,128)} %refs_2_.1, s32[128,1]{1,0:T(8,128)} %copy.49.refs_3_, f32[2,4,2048]{2,1,0:T(4,128)} %refs_4_.1, ...), custom_call_target="tpu_custom_call" | custom-call | tf_op jit(solution)/shard_map/train/pallas_call | solution.py:600
  191.8 0.8 constant_dynamic-slice_fusion
  192.6 0.1 copy.52
  192.7 0.1 reshape.45
  192.8 0.6 multiply_subtract_fusion.2
  193.4 0.8 slice_bitcast_fusion.1
  194.3 0.0 copy-start.9
  194.3 0.8 copy-done.9
  195.1 0.0 copy-done.2
  195.2 0.0 copy-done.8
  195.2 0.8 multiply_subtract_fusion.1
  196.0 0.2 copy-done
  196.1 0.1 copy-done.5
  196.2 0.1 copy-done.6
  196.3 0.9 multiply_subtract_fusion
  197.2 0.7 copy.65
  197.9 0.3 copy-done.1
  198.2 0.7 copy.66
  (24 shorter events, 0.1 us)
Async XLA Ops:
  0.6 0.7 copy-start.10
  1.5 0.7 copy-start.13
  2.2 0.7 copy-start.4
  2.9 189.9 %copy-start.11 = (f32[2,12,4]{1,2,0:T(4,128)S(1)}, f32[2,12,4]{1,2,0:T(4,128)}, u32[]{:S(2)}) copy-start(f32[2,12,4]{1,2,0:T(4,128)} %param.23) | copy-start | bytes 1156
  2.9 189.9 %copy-start.12 = (f32[2,12,4]{1,2,0:T(4,128)S(1)}, f32[2,12,4]{1,2,0:T(4,128)}, u32[]{:S(2)}) copy-start(f32[2,12,4]{1,2,0:T(4,128)} %param.20) | copy-start | bytes 1156
  191.8 2.5 %copy-start.3 = (f32[4,2,4,1536]{3,2,1,0:T(4,128)S(1)}, f32[4,2,4,1536]{3,2,1,0:T(4,128)}, u32[]{:S(2)}) copy-start(f32[4,2,4,1536]{3,2,1,0:T(4,128)} %get-tuple-element.17) | copy-start | bytes 589828
  194.3 0.8 copy-start.9
  194.3 0.9 copy-start.2
  194.3 0.9 copy-start.8
  195.2 0.9 copy-start
  195.2 1.0 copy-start.5
  195.2 1.1 copy-start.6
  196.3 0.9 copy-start.7
  197.2 1.0 copy-start.1

commit v2 on v1

v2 whole, which is shorter than its diff:
```python
import math

import jax
import jax.numpy as jnp
from jax import lax
from jax.experimental import pallas as pl
from jax.experimental.pallas import tpu as pltpu
from jax.sharding import PartitionSpec as P

STEP = 10
NORM_EPSILON = 1e-06
ADAM_EPSILON = 1e-06
BETA_FIRST = 0.9
BETA_SECOND = 0.999
LEARN_RATE = 0.03
VECTOR_RATE = 0.2
WEIGHT_DECAY = 0.01
MASKED_SCORE = -1e30
VMEM_BYTES = 62 * 2**20
MESH = pl.DeviceIdType.MESH
BF = jnp.bfloat16
F32 = jnp.float32
THIRDS = (((0, 128), (128, 256), (256, 512)), ((0, 384), (384, 768), (768, 1024)))
WIDTHS = (512, 1024)
ORDERS = (("x", "y", "z"), ("y", "z", "x"), ("z", "x", "y"))


class Place:
    def __init__(self):
        self.dp = lax.axis_index("dp")
        self.seq = lax.axis_index("seq")
        self.core = self.seq % 2
        self.at = {
            "x": ((self.dp // 4) % 2) * 2 + self.seq // 2,
            "y": self.dp // 8,
            "z": self.dp % 4,
        }

    def device(self, at, core):
        return {
            "dp": (at["y"] * 2 + at["x"] // 2) * 4 + at["z"],
            "seq": (at["x"] % 2) * 2 + core,
        }

    def along(self, axis, step):
        at = dict(self.at)
        at[axis] = (at[axis] + step) % 4
        return at[axis], self.device(at, self.core)

    def other_core(self):
        return self.device(self.at, 1 - self.core)

    def in_group(self, step):
        peer = (self.seq + step) % 4
        return peer, {"dp": self.dp, "seq": peer}


def region(buf, layer, at, core, columns):
    whole = slice(None)
    if "x" in at:
        x_hi, x_lo = at["x"] // 2, at["x"] % 2
    else:
        x_hi, x_lo = whole, whole
    cols = pl.ds(columns[0], columns[1] - columns[0])
    return buf.at[layer, x_lo, core, at.get("y", whole), x_hi, at.get("z", whole), whole, cols]


def greet(place):
    barrier = pltpu.get_barrier_semaphore()
    peers = [place.other_core()]
    for axis in ("x", "y", "z"):
        for step in (1, 2, 3):
            peers.append(place.along(axis, step)[1])
    far = {"dp": place.dp, "seq": (1 - place.seq // 2) * 2 + (1 - place.core)}
    peers.append(far)
    for peer in peers:
        pl.semaphore_signal(barrier, inc=1, device_id=peer, device_id_type=MESH)
    pl.semaphore_wait(barrier, len(peers))


def remote(src, dst, send, recv, device):
    return pltpu.make_async_remote_copy(
        src_ref=src, dst_ref=dst, send_sem=send, recv_sem=recv, device_id=device, device_id_type=MESH
    )


class Table:
    ROUNDS = (("core", (1,)), ("x", (1, 2, 3)), ("y", (1, 2, 3)), ("z", (1, 2, 3)))

    def __init__(self, place, total, came, send, recv):
        self.place, self.total, self.came, self.send, self.recv = place, total, came, send, recv
        self.going = None

    def start(self, number):
        axis, steps = self.ROUNDS[number]
        self.going = []
        for step in steps:
            device = self.place.other_core() if axis == "core" else self.place.along(axis, step)[1]
            copy = remote(
                self.total,
                self.came.at[number, step - 1],
                self.send.at[number, step - 1],
                self.recv.at[number, step - 1],
                device,
            )
            copy.start()
            self.going.append(copy)

    def finish(self, number):
        for copy in self.going:
            copy.wait()
        total = self.total[...]
        for step in self.ROUNDS[number][1]:
            total = total + self.came[number, step - 1]
        self.total[...] = total


def dims_of(axes):
    out = ()
    if "x" in axes:
        out += (2,)
    if "y" in axes:
        out += (4,)
    if "x" in axes:
        out += (2,)
    if "z" in axes:
        out += (4,)
    return out


def each_block(dims, body):
    count = 1
    for size in dims[:-1]:
        count *= size

    def one(i, carry):
        index = ()
        rest = i
        for size in reversed(dims[:-1]):
            index = (rest % size,) + index
            rest = rest // size
        body(index)
        return carry

    if count == 1:
        body(tuple(0 for _ in dims[:-1]))
    else:
        lax.fori_loop(0, count, one, 0)


NT = (((1,), (1,)), ((), ()))
NN = (((1,), (0,)), ((), ()))
TN = (((0,), (0,)), ((), ()))
CHUNKS = ((0, 0), (0, 1), (1, 0), (1, 1))
PIECES = (16, 1536)
SCALE = 0.125
QUARTERS = (0, 3, 1, 2)


def mm(left, right, dims=NN):
    return lax.dot_general(left, right, dims, preferred_element_type=F32)


def column_sum(values):
    return jnp.sum(values, axis=0, keepdims=True)


def normalize(summed):
    center = summed - jnp.mean(summed, axis=-1, keepdims=True)
    spread = jnp.mean(center * center, axis=-1, keepdims=True)
    inverse = lax.rsqrt(spread + NORM_EPSILON)
    return center * inverse, inverse


def normalize_back(grad, hat, inverse):
    mean = jnp.mean(grad, axis=-1, keepdims=True)
    along = jnp.mean(grad * hat, axis=-1, keepdims=True)
    return inverse * (grad - mean - hat * along)


class Gather:
    def __init__(self, place, bufs, send, recv, swap_send, swap_recv):
        self.place, self.bufs = place, bufs
        self.send, self.recv, self.swap_send, self.swap_recv = send, recv, swap_send, swap_recv

    def copies(self, l, arr, phase, coming):
        place = self.place
        out = []
        for j, order in enumerate(ORDERS):
            axis = order[phase]
            here = {a: place.at[a] for a in order[phase:]}
            for step in (1, 2, 3):
                _, device = place.along(axis, step)
                spot = dict(here)
                if coming:
                    spot[axis] = (place.at[axis] - step) % 4
                ref = region(self.bufs[arr], l, spot, place.core, THIRDS[arr][j])
                sems = (self.send.at[l, arr, phase, j, step - 1], self.recv.at[l, arr, phase, j, step - 1])
                out.append(remote(ref, ref, *sems, device))
        return out

    def start(self, l, arr, phase):
        for copy in self.copies(l, arr, phase, False):
            copy.start()
        if phase == 2:
            for j in range(3):
                self.swap(l, arr, j, 0).start()

    def arrive(self, l, arr, phase):
        for copy in self.copies(l, arr, phase, True):
            copy.wait_recv()

    def swap(self, l, arr, j, step, coming=False):
        place = self.place
        axis = ORDERS[j][2]
        core = 1 - place.core if coming else place.core
        ref = region(self.bufs[arr], l, {axis: (place.at[axis] - step) % 4}, core, THIRDS[arr][j])
        return remote(
            ref, ref, self.swap_send.at[l, arr, j, step], self.swap_recv.at[l, arr, j, step], place.other_core()
        )

    def swap_start(self, l, arr):
        copies = self.copies(l, arr, 2, True)
        for step in (1, 3, 2):
            for j in range(3):
                copies[3 * j + step - 1].wait_recv()
                self.swap(l, arr, j, step).start()

    def swap_arrive(self, l, arr):
        for j in range(3):
            for step in range(4):
                self.swap(l, arr, j, step, True).wait_recv()

    def finish(self):
        for chunk in CHUNKS:
            for phase in range(3):
                for copy in self.copies(*chunk, phase, False):
                    copy.wait_send()
            for j in range(3):
                for step in range(4):
                    self.swap(*chunk, j, step).wait_send()


class Scatter:
    def __init__(self, place, bufs, slots, total, send, recv):
        self.place, self.bufs, self.slots, self.total, self.send, self.recv = place, bufs, slots, total, send, recv

    def slot(self, phase, arr, j):
        return self.slots[(phase * 2 + arr) * 3 + j]

    def part(self, l, arr, at, j):
        whole = slice(None)
        x_hi, x_lo = (at["x"] // 2, at["x"] % 2) if "x" in at else (whole, whole)
        low, high = THIRDS[arr][j]
        return self.bufs[arr].at[
            l, x_lo, at.get("y", whole), x_hi, at.get("z", whole), whole, pl.ds(low, high - low)
        ]

    def copies(self, l, arr, phase):
        place = self.place
        out = []
        for j, order in enumerate(ORDERS):
            rev = order[::-1]
            for step in (1, 2, 3):
                there = {a: place.at[a] for a in rev[:phase]}
                there[rev[phase]], device = place.along(rev[phase], step)
                dst = self.slot(phase, arr, j).at[l, step - 1]
                sems = (self.send.at[l, arr, phase, j, step - 1], self.recv.at[l, arr, phase, j, step - 1])
                out.append(remote(self.part(l, arr, there, j), dst, *sems, device))
        return out

    def add_up(self, l, arr, phase):
        for j, order in enumerate(ORDERS):
            rev = order[::-1]
            own = self.part(l, arr, {a: self.place.at[a] for a in rev[: phase + 1]}, j)
            came = self.slot(phase, arr, j)
            if phase == 2:
                low, high = THIRDS[arr][j]
                total = own[...].astype(F32)
                for k in range(3):
                    total = total + came[l, k].astype(F32)
                self.total[l, :, 512 * arr + low : 512 * arr + high] = total
                continue

            def body(index, own=own, came=came):
                total = own[index].astype(F32)
                for k in range(3):
                    total = total + came[(l, k) + index].astype(F32)
                own[index] = total.astype(BF)

            each_block(dims_of(rev[phase + 1 :]), body)

    def step(self, l, arr, stage):
        if stage > 0:
            for copy in self.copies(l, arr, stage - 1):
                copy.wait_recv()
            self.add_up(l, arr, stage - 1)
        if stage < 3:
            for copy in self.copies(l, arr, stage):
                copy.start()

    def finish(self):
        for chunk in CHUNKS:
            for phase in range(3):
                for copy in self.copies(*chunk, phase):
                    copy.wait_send()


def train_kernel(*refs):
    r = dict(zip(NAMES, refs[: len(NAMES)]))
    slots = refs[len(NAMES) :]
    place = Place()
    seq, core, x_lo = place.seq, place.core, place.seq // 2
    peer = 1 - core
    near = place.other_core()
    across = {"dp": place.dp, "seq": (1 - x_lo) * 2 + core}
    wa, wm, ga, gm, vec, vgrad = r["wa"], r["wm"], r["ga"], r["gm"], r["vec"], r["vgrad"]
    s0, r0, stage, kv = r["s0"], r["r0"], r["stage"], r["kv"]
    unsent = []

    def send(src, dst, sem, index, device):
        copy = remote(src, dst, r[sem + "_send"].at[index], r[sem + "_recv"].at[index], device)
        copy.start()
        unsent.append(copy)
        return copy

    for s, q in enumerate(QUARTERS):
        for l in range(2):
            s0[s, l, :, 0:512] = r["w_attn"][l, :, 512 * q : 512 * q + 512]
            s0[s, l, :, 512:1536] = r["w_mlp"][l, :, 1024 * s : 1024 * s + 1024]
    vec[...] = r["table"][...]
    r["docs"][seq] = r["seg_row"][...]
    greet(place)

    pieces, docs = [], []
    for step in (1, 2, 3):
        member, device = place.in_group(step)
        pieces.append(send(s0.at[member], r0.at[seq], "a2a", (0, step), device))
    table = Table(place, vec, r["vgot"].at[0], r["v_send"].at[0], r["v_recv"].at[0])
    table.start(0)
    for step in (1, 2, 3):
        member, device = place.in_group(step)
        docs.append(send(r["docs"].at[seq], r["docs"].at[seq], "doc", step, device))
    r0[seq] = s0[seq]
    for copy in pieces:
        copy.wait_recv()
    for src in range(4):
        for l in range(2):
            stage[l, 4 * src : 4 * src + 4, :] = r0[src, l]
    at = place.at
    for l, arr in CHUNKS:
        block = stage[l, :, 512 * arr : 512 * arr + WIDTHS[arr]].astype(BF)
        (wa, wm)[arr][l, at["x"] % 2, core, at["y"], at["x"] // 2, at["z"]] = block
    gather = Gather(place, (wa, wm), r["ag_send"], r["ag_recv"], r["sw_send"], r["sw_recv"])
    table.finish(0)
    table.start(1)
    for chunk in CHUNKS:
        gather.start(*chunk, 0)
    table.finish(1)
    table.start(2)
    for chunk in CHUNKS[:2]:
        gather.arrive(*chunk, 0)
        gather.start(*chunk, 1)
    table.finish(2)
    table.start(3)
    for chunk in CHUNKS[:2]:
        gather.arrive(*chunk, 1)
        gather.start(*chunk, 2)
    for copy in docs:
        copy.wait_recv()
    seg_row = jnp.concatenate([r["docs"][i] for i in range(4)], axis=1)
    r["bias"][...] = jnp.where(r["seg_col"][...] == seg_row, 0.0, MASKED_SCORE)
    for chunk in CHUNKS[2:]:
        gather.arrive(*chunk, 0)
    table.finish(3)
    gather.swap_start(0, 0)
    gather.swap_arrive(0, 0)

    def weight(l, arr, s, low=0, high=None):
        high = WIDTHS[arr] if high is None else high
        return (wa, wm)[arr][l, s // 2, s % 2, :, :, :, :, low:high].reshape(512, high - low)

    def attn_weight(l, q):
        return weight(l, 0, QUARTERS.index(q))

    def put_grad(l, arr, plane, left, right, parts):
        width = WIDTHS[arr] // parts
        for i in range(parts):
            value = mm(left, right(width * i, width * i + width), TN)
            (ga, gm)[arr][l, plane, :, :, :, :, width * i : width * i + width] = value.astype(BF).reshape(
                4, 2, 4, 16, width
            )

    def row(l, k):
        return vec[12 * l + k : 12 * l + k + 1, :]

    def put_row(l, k, value):
        vgrad[12 * l + k : 12 * l + k + 1, :] = value

    lanes = lax.broadcasted_iota(jnp.int32, (1, 128), 1)
    first = (lanes < 64).astype(F32)
    second = 1.0 - first
    first_low, second_low = first.astype(BF), second.astype(BF)

    def both(pair):
        return jnp.concatenate([pair * first_low, pair * second_low], axis=0)

    def joined(stacked):
        return stacked[:128] * first + stacked[128:] * second

    def group_rows(l, which, low):
        return kv[l, :, which, :, low : low + 128].reshape(512, 128)

    def put_keys(l, which, value):
        kv[l, seq, which] = value.astype(BF)
        mine = kv.at[l, seq, which]
        far = send(mine, mine, "kv", (l, which, 0), across)
        return far, send(mine, mine, "kv", (l, which, 1), near)

    def pass_on(l, which, far):
        far.wait_recv()
        came = kv.at[l, (1 - x_lo) * 2 + core, which]
        return send(came, came, "kv", (l, which, 2), near)

    pairs = r["pairs"]
    hidden = r["tokens"][...].astype(F32)
    for l in range(2):
        if l == 1:
            gather.swap_arrive(1, 0)
        low_in = hidden.astype(BF)
        pairs[l, 0, core] = low_in
        send(pairs.at[l, 0, core], pairs.at[l, 0, core], "act", (l, 0), near)
        keys_way = put_keys(l, 0, mm(low_in, attn_weight(l, 1)))
        values_way = put_keys(l, 1, mm(low_in, attn_weight(l, 2)) + row(l, 1))
        r["q"][l] = (mm(low_in, attn_weight(l, 0)) + row(l, 0)).astype(BF)
        if l == 0:
            for chunk in CHUNKS[2:]:
                gather.start(*chunk, 1)
            gather.swap_start(0, 1)
        on_keys = pass_on(l, 0, keys_way[0])
        on_values = pass_on(l, 1, values_way[0])
        if l == 0:
            for chunk in CHUNKS[2:]:
                gather.arrive(*chunk, 1)
                gather.start(*chunk, 2)
        for copy in (keys_way[1], values_way[1], on_keys, on_values):
            copy.wait_recv()
        for pair in range(4):
            low = 128 * pair
            scores = mm(both(r["q"][l, :, low : low + 128]), group_rows(l, 0, low), NT) * SCALE
            bias = r["bias"][...]
            scores = scores + jnp.concatenate([bias, bias], axis=0)
            powers = jnp.exp(scores - jnp.max(scores, axis=-1, keepdims=True))
            probs = (powers * (1.0 / jnp.sum(powers, axis=-1, keepdims=True))).astype(BF)
            r["probs"][l, pair] = probs
            pairs[l, 1, core, :, low : low + 128] = joined(mm(probs, group_rows(l, 1, low))).astype(BF)
        send(pairs.at[l, 1, core], pairs.at[l, 1, core], "act", (l, 1), near)
        if l == 0:
            gather.swap_arrive(0, 1)
        hat, inverse = normalize(hidden + mm(pairs[l, 1, core], attn_weight(l, 3)) + row(l, 2))
        r["hat1"][l] = hat
        r["inv1"][l] = inverse
        normed = hat * row(l, 3) + row(l, 4)
        low_normed = normed.astype(BF)
        pairs[l, 2, core] = low_normed
        send(pairs.at[l, 2, core], pairs.at[l, 2, core], "act", (l, 2), near)
        back = jnp.zeros((128, 512), F32)
        if l == 1:
            gather.swap_start(1, 1)
            gather.swap_arrive(1, 1)
        for i in range(4):
            half, low = i // 2, 512 * (i % 2)
            pre = mm(low_normed, weight(l, 1, half, low, low + 512)) + row(l, 5 + i)
            normal = 0.5 + 0.5 * lax.erf(pre * (0.5**0.5))
            act = (pre * normal).astype(BF)
            r["act"][l, half, core, :, low : low + 512] = act
            slope = normal + pre * (jnp.exp(pre * pre * -0.5) * (1.0 / (2.0 * math.pi) ** 0.5))
            r["slope"][l, :, 512 * i : 512 * i + 512] = slope.astype(BF)
            back = back + mm(act, weight(l, 1, 2 + half, low, low + 512), NT)
        mine = r["act"].at[l, peer, core]
        send(mine, mine, "act", (l, 3), near)
        if l == 0:
            gather.swap_start(1, 0)
        hat, inverse = normalize(normed + back + row(l, 9))
        r["hat2"][l] = hat
        r["inv2"][l] = inverse
        hidden = hat * row(l, 10) + row(l, 11)
    r["block_out"][...] = hidden.astype(BF)

    scatter = Scatter(place, (ga, gm), slots, r["total"], r["rs_send"], r["rs_recv"])
    dkv, dkv_near, dkv_far, late, early = r["dkv"], r["dkv_near"], r["dkv_far"], r["late"], r["early"]

    def halves(part):
        return pl.ds(256 * part, 256)

    def give_near(l, part):
        return send(
            dkv.at[l, :, peer, :, :, halves(part)], dkv_near.at[l, :, :, :, halves(part)], "dkv", (l, part, 0), near
        )

    def give_far(l, part, copy):
        copy.wait_recv()
        span = slice(256 * part, 256 * part + 256)
        mine = dkv[l, 1 - x_lo, core, :, :, span].astype(F32) + dkv_near[l, 1 - x_lo, :, :, span].astype(F32)
        dkv[l, 1 - x_lo, core, :, :, span] = mine.astype(BF)
        return send(
            dkv.at[l, 1 - x_lo, core, :, :, halves(part)], dkv_far.at[l, :, :, halves(part)], "dkv", (l, part, 1), across
        )

    def act_arrive(l, which):
        if which == 3:
            ref = r["act"].at[l, core, peer]
        else:
            ref = pairs.at[l, which, peer]
        remote(ref, ref, r["act_send"].at[l, which], r["act_recv"].at[l, which], near).wait_recv()

    def two(ref, *index):
        return ref[index].reshape(256, -1)

    grad = r["cotangent"][...].astype(F32)
    for l in (1, 0):
        hat = r["hat2"][l]
        put_row(l, 10, column_sum(grad * hat))
        put_row(l, 11, column_sum(grad))
        grad_second = normalize_back(grad * row(l, 10), hat, r["inv2"][l])
        put_row(l, 9, column_sum(grad_second))
        low_second = grad_second.astype(BF)
        pairs[l, 3, core] = low_second
        got_second = send(pairs.at[l, 3, core], pairs.at[l, 3, core], "back", (l, 0), near)
        grad_normed = grad_second
        for i in range(4):
            half, low = i // 2, 512 * (i % 2)
            grad_act = mm(low_second, weight(l, 1, 2 + half, low, low + 512))
            grad_pre = (grad_act * r["slope"][l, :, 512 * i : 512 * i + 512].astype(F32)).astype(BF)
            put_row(l, 5 + i, column_sum(grad_pre.astype(F32)))
            r["du"][l, half, core, :, low : low + 512] = grad_pre
            grad_normed = grad_normed + mm(grad_pre, weight(l, 1, half, low, low + 512), NT)
        mine = r["du"].at[l, peer, core]
        send(mine, mine, "back", (l, 1), near)
        if l == 0:
            scatter.step(1, 1, 1)
        hat = r["hat1"][l]
        put_row(l, 3, column_sum(grad_normed * hat))
        put_row(l, 4, column_sum(grad_normed))
        grad_first = normalize_back(grad_normed * row(l, 3), hat, r["inv1"][l])
        put_row(l, 2, column_sum(grad_first))
        low_first = grad_first.astype(BF)
        early[l, 1, core] = low_first
        grad_mixed = mm(low_first, attn_weight(l, 3), NT).astype(BF)
        near_ways, far_ways = [], []
        for pair in range(4):
            low = 128 * pair
            keys, values = group_rows(l, 0, low), group_rows(l, 1, low)
            grad_pair = both(grad_mixed[:, low : low + 128])
            probs = r["probs"][l, pair]
            grad_probs = mm(grad_pair, values, NT)
            dkv[l, :, :, 1, :, low : low + 128] = mm(probs, grad_pair, TN).astype(BF).reshape(2, 2, 128, 128)
            wide = probs.astype(F32)
            row_dot = jnp.sum(grad_probs * wide, axis=-1, keepdims=True)
            grad_scores = (wide * (grad_probs - row_dot)).astype(BF)
            early[l, 0, core, :, low : low + 128] = (joined(mm(grad_scores, keys)) * SCALE).astype(BF)
            grad_keys = mm(grad_scores, both(r["q"][l, :, low : low + 128]), TN) * SCALE
            dkv[l, :, :, 0, :, low : low + 128] = grad_keys.astype(BF).reshape(2, 2, 128, 128)
            if pair % 2 == 1:
                near_ways.append(give_near(l, pair // 2))
            if pair == 2:
                far_ways.append(give_far(l, 0, near_ways[0]))
        mine = early.at[l, peer, core]
        send(mine, mine, "back", (l, 2), near)
        grad_queries = early[l, 0, core]
        put_row(l, 0, column_sum(grad_queries.astype(F32)))
        grad = grad_first + mm(grad_queries, attn_weight(l, 0), NT)
        far_ways.append(give_far(l, 1, near_ways[1]))
        if l == 0:
            scatter.step(1, 0, 1)
        got_second.wait_recv()
        act_arrive(l, 2)
        act_arrive(l, 3)
        theirs = r["du"].at[l, core, peer]
        remote(theirs, theirs, r["back_send"].at[l, 1], r["back_recv"].at[l, 1], near).wait_recv()
        put_grad(l, 1, 0, two(pairs, l, 2), lambda low, high: r["du"][l, core, :, :, low:high].reshape(256, -1), 2)
        put_grad(l, 1, 1, two(pairs, l, 3), lambda low, high: r["act"][l, core, :, :, low:high].reshape(256, -1), 2)
        scatter.step(l, 1, 0)
        act_arrive(l, 0)
        act_arrive(l, 1)
        theirs = early.at[l, core, peer]
        remote(theirs, theirs, r["back_send"].at[l, 2], r["back_recv"].at[l, 2], near).wait_recv()
        put_grad(l, 0, 0, two(pairs, l, core), lambda low, high: two(early, l, core), 1)
        if l == 0:
            scatter.step(1, 1, 2)
            scatter.step(1, 0, 2)
        for copy in far_ways:
            copy.wait_recv()
        for which in range(2):
            total = dkv[l, x_lo, core, which].astype(F32) + dkv_near[l, x_lo, which].astype(F32)
            late[l, which, core] = (total + dkv_far[l, which].astype(F32)).astype(BF)
        mine = late.at[l, peer, core]
        send(mine, mine, "back", (l, 3), near)
        put_row(l, 1, column_sum(late[l, 1, core].astype(F32)))
        if l == 0:
            table = Table(place, vgrad, r["vgot"].at[1], r["v_send"].at[1], r["v_recv"].at[1])
            table.start(0)
        grad = grad + mm(late[l, 0, core], attn_weight(l, 1), NT) + mm(late[l, 1, core], attn_weight(l, 2), NT)
        theirs = late.at[l, core, peer]
        remote(theirs, theirs, r["back_send"].at[l, 3], r["back_recv"].at[l, 3], near).wait_recv()
        put_grad(l, 0, 1, two(pairs, l, 0), lambda low, high: two(late, l, core), 1)
        if l == 0:
            table.finish(0)
            table.start(1)
        scatter.step(l, 0, 0)
    r["input_grad"][...] = grad
    scatter.step(1, 1, 3)
    scatter.step(1, 0, 3)
    table.finish(1)
    table.start(2)
    scatter.step(0, 1, 1)
    scatter.step(0, 0, 1)
    table.finish(2)
    table.start(3)
    scatter.step(0, 1, 2)
    scatter.step(0, 0, 2)
    table.finish(3)
    scatter.step(0, 1, 3)
    scatter.step(0, 0, 3)
    s4, fin, total = r["s4"], r["fin"], r["total"]
    for dst in range(4):
        for l in range(2):
            s4[dst, l] = total[l, 4 * dst : 4 * dst + 4, :]
    moved = []
    for step in (1, 2, 3):
        member, device = place.in_group(step)
        moved.append(send(s4.at[member], fin.at[seq], "a2a", (1, step), device))
    fin[seq] = s4[seq]
    gather.finish()
    scatter.finish()
    for copy in moved:
        copy.wait_recv()
    for copy in unsent:
        copy.wait_send()


INPUTS = ("tokens", "cotangent", "seg_row", "seg_col", "w_attn", "w_mlp", "table")
OUTPUTS = {
    "block_out": ((128, 512), BF),
    "input_grad": ((128, 512), F32),
    "fin": ((4, 2, 4, 1536), F32),
    "vgrad": ((24, 512), F32),
}
DIMS = (2, 2, 2, 4, 2, 4, 16)
HALF = (2, 2, 4, 2, 4, 16)
SCRATCH = {
    "wa": (DIMS + (512,), BF),
    "wm": (DIMS + (1024,), BF),
    "ga": (HALF + (512,), BF),
    "gm": (HALF + (1024,), BF),
    "vec": ((24, 512), F32),
    "s0": ((4, 2, 4, 1536), F32),
    "r0": ((4, 2, 4, 1536), F32),
    "s4": ((4, 2, 4, 1536), F32),
    "stage": ((2, 16, 1536), F32),
    "total": ((2, 16, 1536), F32),
    "vgot": ((2, 4, 3, 24, 512), F32),
    "docs": ((4, 1, 128), jnp.int32),
    "bias": ((128, 512), F32),
    "q": ((2, 128, 512), BF),
    "kv": ((2, 4, 2, 128, 512), BF),
    "probs": ((2, 4, 256, 512), BF),
    "pairs": ((2, 4, 2, 128, 512), BF),
    "act": ((2, 2, 2, 128, 1024), BF),
    "du": ((2, 2, 2, 128, 1024), BF),
    "early": ((2, 2, 2, 128, 512), BF),
    "late": ((2, 2, 2, 128, 512), BF),
    "hat1": ((2, 128, 512), F32),
    "inv1": ((2, 128, 1), F32),
    "slope": ((2, 128, 2048), BF),
    "hat2": ((2, 128, 512), F32),
    "inv2": ((2, 128, 1), F32),
    "dkv": ((2, 2, 2, 2, 128, 512), BF),
    "dkv_near": ((2, 2, 2, 128, 512), BF),
    "dkv_far": ((2, 2, 128, 512), BF),
}
SEMS = {
    "a2a": (2, 4),
    "doc": (4,),
    "ag": (2, 2, 3, 3, 3),
    "sw": (2, 2, 3, 4),
    "rs": (2, 2, 3, 3, 3),
    "kv": (2, 2, 3),
    "dkv": (2, 2, 2),
    "act": (2, 4),
    "back": (2, 4),
    "v": (2, 4, 3),
}
NAMES = INPUTS + tuple(OUTPUTS) + tuple(SCRATCH) + tuple(f"{n}_{d}" for n in SEMS for d in ("send", "recv"))


def train(*args):
    slots = []
    for phase in range(3):
        for arr in range(2):
            for j in range(3):
                low, high = THIRDS[arr][j]
                rest = dims_of(ORDERS[j][::-1][phase + 1 :])
                slots.append(pltpu.VMEM((2, 3) + rest + (16, high - low), BF))
    scratch = [pltpu.VMEM(*spec) for spec in SCRATCH.values()]
    for shape in SEMS.values():
        scratch += [pltpu.SemaphoreType.DMA(shape)] * 2
    return pl.pallas_call(
        train_kernel,
        out_shape=tuple(jax.ShapeDtypeStruct(*spec) for spec in OUTPUTS.values()),
        in_specs=[pl.BlockSpec(memory_space=pltpu.VMEM)] * len(INPUTS),
        out_specs=[pl.BlockSpec(memory_space=pltpu.VMEM)] * len(OUTPUTS),
        scratch_shapes=scratch + slots,
        compiler_params=pltpu.CompilerParams(
            collective_id=0, has_side_effects=True, vmem_limit_bytes=VMEM_BYTES
        ),
        name="train",
    )(*args)


def adam_update(weight, grad, first, second, rate, decay):
    first_new = BETA_FIRST * first + (1.0 - BETA_FIRST) * grad
    second_new = BETA_SECOND * second + (1.0 - BETA_SECOND) * grad * grad
    first_fix = 1.0 - BETA_FIRST**STEP
    second_fix = 1.0 - BETA_SECOND**STEP
    weight_new = weight - rate * (
        first_new / first_fix / (jnp.sqrt(second_new / second_fix) + ADAM_EPSILON) + decay * weight
    )
    return (first_new, second_new, weight_new)


def local(
    tokens, cotangent, segments, w_attn, w_mlp, vectors, m_attn, m_mlp, m_vec, v_attn, v_mlp, v_vec
):
    place = lax.axis_index("dp") * 4 + lax.axis_index("seq")
    table = lax.dynamic_update_slice(
        jnp.zeros((24, 512), F32),
        vectors.astype(BF).astype(F32).reshape(24, 4),
        (0, 4 * place),
    )
    block_out, input_grad, fin, vec_total = train(
        tokens[0], cotangent[0], segments, segments.reshape(128, 1), w_attn, w_mlp, table
    )
    grad_attn = jnp.concatenate([fin[QUARTERS.index(q), ..., :512] for q in range(4)], axis=-1)
    grad_mlp = fin[..., 512:].transpose(1, 2, 0, 3).reshape(2, 4, 4096)
    grad_vec = lax.dynamic_slice(vec_total, (0, 4 * place), (24, 4)).reshape(2, 12, 4)
    return (
        block_out[None],
        input_grad[None],
        *adam_update(w_attn, grad_attn, m_attn, v_attn, LEARN_RATE, WEIGHT_DECAY),
        *adam_update(w_mlp, grad_mlp, m_mlp, v_mlp, LEARN_RATE, WEIGHT_DECAY),
        *adam_update(vectors, grad_vec, m_vec, v_vec, VECTOR_RATE, 0.0),
    )


def solution(mesh):
    in_specs = (
        P("dp", "seq", None),
        P("dp", "seq", None),
        P("dp", "seq"),
        P(None, ("dp", "seq"), None),
        P(None, ("dp", "seq"), None),
        P(None, None, ("dp", "seq")),
        P(None, ("dp", "seq"), None),
        P(None, ("dp", "seq"), None),
        P(None, None, ("dp", "seq")),
        P(None, ("dp", "seq"), None),
        P(None, ("dp", "seq"), None),
        P(None, None, ("dp", "seq")),
    )
    out_specs = (
        P("dp", "seq", None),
        P("dp", "seq", None),
        P(None, ("dp", "seq"), None),
        P(None, ("dp", "seq"), None),
        P(None, ("dp", "seq"), None),
        P(None, ("dp", "seq"), None),
        P(None, ("dp", "seq"), None),
        P(None, ("dp", "seq"), None),
        P(None, None, ("dp", "seq")),
        P(None, None, ("dp", "seq")),
        P(None, None, ("dp", "seq")),
    )
    return jax.shard_map(local, mesh=mesh, in_specs=in_specs, out_specs=out_specs, check_vma=False)
```

time: 199 us -> 146 us (0.73)
  Pallas kernels: 189 us -> 135 us
    pallas_call x1, Pallas kernels: 189 us -> 135 us  [train(): pl.pallas_call(train_kernel, out_shape=tuple((jax.ShapeDtypeStruct(*spec)...]
    unnamed x32 -> x31, local copies, waits for them, and re-layouts: 4.66 us -> 3.82 us
where the time goes in v2:
time: 146 us; the launch traced here: 145 us
  Pallas kernels  135 us (92%)
  local copies, waits for them, and re-layouts  6.94 us (5%)
  other arithmetic  2.32 us (2%)
    pallas_call x1, Pallas kernels, train(): pl.pallas_call(train_kernel, out_shape=tuple((jax.ShapeDtypeStruct(*spec)...  135 us
    unnamed x31, local copies, waits for them, and re-layouts  3.82 us

profile of v2, /device:TPU:1, one launch (start us, length us, event | category | flops | bytes accessed | tf_op | source)
XLA Modules:
  0.0 145.4 jit_solution(1388564524541146309)
XLA Ops:
  0.7 0.7 copy-done.10
  1.3 0.1 reshape.43
  1.4 0.1 copy.47
  1.5 0.4 dynamic_update_slice.3.refs_6_
  2.0 0.2 copy-done.13
  2.2 0.7 copy.48.refs_3_
  2.9 135.4 %train.1 = (bf16[128,512]{1,0:T(8,128)(2,1)}, f32[128,512]{1,0:T(8,128)}, f32[4,2,4,1536]{3,2,1,0:T(4,128)}, f32[24,512]{1,0:T(8,128)}) custom-call(bf16[128,512]{1,0:T(8,128)(2,1)} %bitcast.24, bf16[128,512]{1,0:T(8,128)(2,1)} %bitcast.25, s32[1,128]{1,0:T(1,128)} %refs_2_.1, s32[128,1]{1,0:T(8,128)} %copy.48.refs_3_, f32[2,4,2048]{2,1,0:T(4,128)} %refs_4_.1, ...), custom_call_target="tpu_custom_call" | custom-call | tf_op jit(solution)/shard_map/train/pallas_call | solution.py:708
  138.3 0.8 constant_dynamic-slice_fusion
  139.2 0.1 copy.50
  139.2 0.1 reshape.41
  139.3 0.6 multiply_subtract_fusion.2
  139.9 0.8 slice_bitcast_fusion.4
  140.7 0.0 copy-start.2
  140.8 0.8 copy-done.2
  141.6 0.0 copy-done.8
  141.6 0.0 copy-done.9
  141.7 0.8 multiply_subtract_fusion.1
  142.4 0.1 copy-done
  142.6 0.1 copy-done.5
  142.7 0.1 copy-done.6
  142.8 0.9 multiply_subtract_fusion
  143.7 0.7 copy.62
  144.3 0.3 copy-done.1
  144.7 0.7 copy.63
  (23 shorter events, 0.1 us)
Async XLA Ops:
  0.6 0.7 copy-start.10
  1.5 0.7 copy-start.13
  2.2 0.7 copy-start.4
  2.9 136.4 %copy-start.11 = (f32[2,12,4]{1,2,0:T(4,128)S(1)}, f32[2,12,4]{1,2,0:T(4,128)}, u32[]{:S(2)}) copy-start(f32[2,12,4]{1,2,0:T(4,128)} %param.23) | copy-start | bytes 1156
  2.9 136.4 %copy-start.12 = (f32[2,12,4]{1,2,0:T(4,128)S(1)}, f32[2,12,4]{1,2,0:T(4,128)}, u32[]{:S(2)}) copy-start(f32[2,12,4]{1,2,0:T(4,128)} %param.20) | copy-start | bytes 1156
  138.3 2.4 %copy-start.3 = (f32[4,2,4,1536]{3,2,1,0:T(4,128)S(1)}, f32[4,2,4,1536]{3,2,1,0:T(4,128)}, u32[]{:S(2)}) copy-start(f32[4,2,4,1536]{3,2,1,0:T(4,128)} %get-tuple-element.17) | copy-start | bytes 589828
  140.7 0.8 copy-start.2
  140.8 0.9 copy-start.8
  140.8 0.9 copy-start.9
  141.7 0.9 copy-start
  141.7 1.0 copy-start.5
  141.7 1.1 copy-start.6
  142.8 0.9 copy-start.7
  143.7 1.0 copy-start.1

commit v3 on v2

--- a/solution.py
+++ b/solution.py
@@ -85,34 +85,36 @@
 
 
 class Table:
-    ROUNDS = (("core", (1,)), ("x", (1, 2, 3)), ("y", (1, 2, 3)), ("z", (1, 2, 3)))
-
-    def __init__(self, place, total, came, send, recv):
-        self.place, self.total, self.came, self.send, self.recv = place, total, came, send, recv
-        self.going = None
-
-    def start(self, number):
-        axis, steps = self.ROUNDS[number]
-        self.going = []
+    ROUNDS = {"core": (0, (1,)), "x": (1, (1, 2, 3)), "y": (2, (1, 2, 3)), "z": (3, (1, 2, 3))}
+
+    def __init__(self, place, blocks, came, send, recv):
+        self.place, self.blocks, self.came, self.send, self.recv = place, blocks, came, send, recv
+        self.going, self.mode, self.axis = None, None, None
+
+    def start(self, axis, mode="add"):
+        number, steps = self.ROUNDS[axis]
+        own = self.blocks.at[self.place.at["y"]]
+        self.going, self.mode, self.axis = [], mode, axis
         for step in steps:
-            device = self.place.other_core() if axis == "core" else self.place.along(axis, step)[1]
-            copy = remote(
-                self.total,
-                self.came.at[number, step - 1],
-                self.send.at[number, step - 1],
-                self.recv.at[number, step - 1],
-                device,
-            )
+            if axis == "core":
+                device = self.place.other_core()
+            else:
+                pos, device = self.place.along(axis, step)
+            src = self.blocks.at[pos] if mode == "collect" else own
+            dst = own if mode == "spread" else self.came.at[number, step - 1]
+            copy = remote(src, dst, self.send.at[number, step - 1], self.recv.at[number, step - 1], device)
             copy.start()
             self.going.append(copy)
 
-    def finish(self, number):
+    def finish(self):
+        number, steps = self.ROUNDS[self.axis]
         for copy in self.going:
             copy.wait()
-        total = self.total[...]
-        for step in self.ROUNDS[number][1]:
-            total = total + self.came[number, step - 1]
-        self.total[...] = total
+        if self.mode != "spread":
+            total = self.blocks[self.place.at["y"]]
+            for step in steps:
+                total = total + self.came[number, step - 1]
+            self.blocks[self.place.at["y"]] = total
 
 
 def dims_of(axes):
@@ -324,20 +326,30 @@
         unsent.append(copy)
         return copy
 
+    t0 = r["t0"]
     for s, q in enumerate(QUARTERS):
         for l in range(2):
-            s0[s, l, :, 0:512] = r["w_attn"][l, :, 512 * q : 512 * q + 512]
-            s0[s, l, :, 512:1536] = r["w_mlp"][l, :, 1024 * s : 1024 * s + 1024]
-    vec[...] = r["table"][...]
-    r["docs"][seq] = r["seg_row"][...]
+            t0[s, 8 * l : 8 * l + 4, 0:512] = r["w_attn"][l, :, 512 * q : 512 * q + 512]
+            t0[s, 8 * l : 8 * l + 4, 512:768] = r["w_mlp"][l, :, 1024 * s : 1024 * s + 256]
+            t0[s, 8 * l + 4 : 8 * l + 8, :] = r["w_mlp"][l, :, 1024 * s + 256 : 1024 * s + 1024]
+    s0[...] = t0[...].astype(BF)
+    tab = r["tab"]
+    number = place.dp * 4 + seq
+    tab[place.at["y"]] = jnp.zeros((24, 128), F32)
+    for l in range(2):
+        tab[place.at["y"], 12 * l : 12 * l + 12, 0:4] = r["vectors"][l].astype(BF).astype(F32)
+    tab[place.at["y"]] = pltpu.roll(tab[place.at["y"]], 4 * (number % 32), 1)
+    r["docs"][seq] = r["segments"][...]
+    xall = r["xall"]
+    xall[0, x_lo, core] = r["tokens"][...]
     greet(place)
 
     pieces, docs = [], []
     for step in (1, 2, 3):
         member, device = place.in_group(step)
-        pieces.append(send(s0.at[member], r0.at[seq], "a2a", (0, step), device))
-    table = Table(place, vec, r["vgot"].at[0], r["v_send"].at[0], r["v_recv"].at[0])
-    table.start(0)
+        pieces.append(send(s0.at[member], r0.at[seq], "a2a", (2, step), device))
+    table = Table(place, tab, r["vgot"].at[0], r["v_send"].at[0], r["v_recv"].at[0])
+    table.start("core")
     for step in (1, 2, 3):
         member, device = place.in_group(step)
         docs.append(send(r["docs"].at[seq], r["docs"].at[seq], "doc", step, device))
@@ -345,35 +357,56 @@
     for copy in pieces:
         copy.wait_recv()
     for src in range(4):
+        t0[src] = r0[src].astype(F32)
         for l in range(2):
-            stage[l, 4 * src : 4 * src + 4, :] = r0[src, l]
+            stage[l, 4 * src : 4 * src + 4, 0:768] = t0[src, 8 * l : 8 * l + 4, :]
+            stage[l, 4 * src : 4 * src + 4, 768:1536] = t0[src, 8 * l + 4 : 8 * l + 8, :]
     at = place.at
     for l, arr in CHUNKS:
         block = stage[l, :, 512 * arr : 512 * arr + WIDTHS[arr]].astype(BF)
         (wa, wm)[arr][l, at["x"] % 2, core, at["y"], at["x"] // 2, at["z"]] = block
     gather = Gather(place, (wa, wm), r["ag_send"], r["ag_recv"], r["sw_send"], r["sw_recv"])
-    table.finish(0)
-    table.start(1)
+    table.finish()
+    table.start("x")
     for chunk in CHUNKS:
         gather.start(*chunk, 0)
-    table.finish(1)
-    table.start(2)
-    for chunk in CHUNKS[:2]:
+
+    def share(l):
+        mine = xall.at[l, x_lo, core]
+        near_way = send(mine, mine, "x", (l, 0), near)
+        return near_way, send(mine, mine, "x", (l, 1), across)
+
+    def pass_on(l, far_way):
+        far_way.wait_recv()
+        came = xall.at[l, 1 - x_lo, core]
+        return send(came, came, "x", (l, 2), near)
+
+    first_near, first_far = share(0)
+    table.finish()
+    table.start("z")
+    for chunk in CHUNKS:
         gather.arrive(*chunk, 0)
         gather.start(*chunk, 1)
-    table.finish(2)
-    table.start(3)
+    table.finish()
+    table.start("y", "spread")
     for chunk in CHUNKS[:2]:
         gather.arrive(*chunk, 1)
         gather.start(*chunk, 2)
+    first_on = pass_on(0, first_far)
     for copy in docs:
         copy.wait_recv()
-    seg_row = jnp.concatenate([r["docs"][i] for i in range(4)], axis=1)
-    r["bias"][...] = jnp.where(r["seg_col"][...] == seg_row, 0.0, MASKED_SCORE)
+    own_docs = jnp.broadcast_to(r["docs"][seq].astype(F32), (128, 128)).T
+    for i in range(4):
+        r["bias"][:, 128 * i : 128 * i + 128] = jnp.where(own_docs == r["docs"][i].astype(F32), 0.0, MASKED_SCORE)
+    table.finish()
+    for y in range(4):
+        vec[:, 128 * y : 128 * y + 128] = tab[y]
+    gather.swap_start(0, 0)
     for chunk in CHUNKS[2:]:
-        gather.arrive(*chunk, 0)
-    table.finish(3)
-    gather.swap_start(0, 0)
+        gather.arrive(*chunk, 1)
+        gather.start(*chunk, 2)
+    first_near.wait_recv()
+    first_on.wait_recv()
     gather.swap_arrive(0, 0)
 
     def weight(l, arr, s, low=0, high=None):
@@ -409,42 +442,31 @@
         return stacked[:128] * first + stacked[128:] * second
 
     def group_rows(l, which, low):
-        return kv[l, :, which, :, low : low + 128].reshape(512, 128)
-
-    def put_keys(l, which, value):
-        kv[l, seq, which] = value.astype(BF)
-        mine = kv.at[l, seq, which]
-        far = send(mine, mine, "kv", (l, which, 0), across)
-        return far, send(mine, mine, "kv", (l, which, 1), near)
-
-    def pass_on(l, which, far):
-        far.wait_recv()
-        came = kv.at[l, (1 - x_lo) * 2 + core, which]
-        return send(came, came, "kv", (l, which, 2), near)
+        return kv[l, which, :, :, low : low + 128].reshape(512, 128)
+
+    def chip_keys(l, chip):
+        rows = xall[l, chip].reshape(256, 512)
+        kv[l, 0, chip] = mm(rows, attn_weight(l, 1)).astype(BF)
+        kv[l, 1, chip] = (mm(rows, attn_weight(l, 2)) + row(l, 1)).astype(BF)
 
     pairs = r["pairs"]
     hidden = r["tokens"][...].astype(F32)
     for l in range(2):
+        low_in = hidden.astype(BF)
         if l == 1:
+            xall[1, x_lo, core] = low_in
+            near_way, far_way = share(1)
             gather.swap_arrive(1, 0)
-        low_in = hidden.astype(BF)
-        pairs[l, 0, core] = low_in
-        send(pairs.at[l, 0, core], pairs.at[l, 0, core], "act", (l, 0), near)
-        keys_way = put_keys(l, 0, mm(low_in, attn_weight(l, 1)))
-        values_way = put_keys(l, 1, mm(low_in, attn_weight(l, 2)) + row(l, 1))
         r["q"][l] = (mm(low_in, attn_weight(l, 0)) + row(l, 0)).astype(BF)
-        if l == 0:
-            for chunk in CHUNKS[2:]:
-                gather.start(*chunk, 1)
-            gather.swap_start(0, 1)
-        on_keys = pass_on(l, 0, keys_way[0])
-        on_values = pass_on(l, 1, values_way[0])
-        if l == 0:
-            for chunk in CHUNKS[2:]:
-                gather.arrive(*chunk, 1)
-                gather.start(*chunk, 2)
-        for copy in (keys_way[1], values_way[1], on_keys, on_values):
-            copy.wait_recv()
+        if l == 1:
+            near_way.wait_recv()
+        chip_keys(l, x_lo)
+        if l == 1:
+            on_way = pass_on(1, far_way)
+            gather.swap_start(1, 1)
+            on_way.wait_recv()
+        chip_keys(l, 1 - x_lo)
+        pairs[l, 0] = xall[l, x_lo]
         for pair in range(4):
             low = 128 * pair
             scores = mm(both(r["q"][l, :, low : low + 128]), group_rows(l, 0, low), NT) * SCALE
@@ -454,6 +476,8 @@
             probs = (powers * (1.0 / jnp.sum(powers, axis=-1, keepdims=True))).astype(BF)
             r["probs"][l, pair] = probs
             pairs[l, 1, core, :, low : low + 128] = joined(mm(probs, group_rows(l, 1, low))).astype(BF)
+            if l == 0 and pair == 1:
+                gather.swap_start(0, 1)
         send(pairs.at[l, 1, core], pairs.at[l, 1, core], "act", (l, 1), near)
         if l == 0:
             gather.swap_arrive(0, 1)
@@ -466,7 +490,6 @@
         send(pairs.at[l, 2, core], pairs.at[l, 2, core], "act", (l, 2), near)
         back = jnp.zeros((128, 512), F32)
         if l == 1:
-            gather.swap_start(1, 1)
             gather.swap_arrive(1, 1)
         for i in range(4):
             half, low = i // 2, 512 * (i % 2)
@@ -488,24 +511,19 @@
     r["block_out"][...] = hidden.astype(BF)
 
     scatter = Scatter(place, (ga, gm), slots, r["total"], r["rs_send"], r["rs_recv"])
-    dkv, dkv_near, dkv_far, late, early = r["dkv"], r["dkv_near"], r["dkv_far"], r["late"], r["early"]
-
-    def halves(part):
-        return pl.ds(256 * part, 256)
-
-    def give_near(l, part):
-        return send(
-            dkv.at[l, :, peer, :, :, halves(part)], dkv_near.at[l, :, :, :, halves(part)], "dkv", (l, part, 0), near
-        )
-
-    def give_far(l, part, copy):
+    dx, dx_near, dx_far, late, early = r["dx"], r["dx_near"], r["dx_far"], r["late"], r["early"]
+
+    def grad_rows(l, chip):
+        keys, values = late[l, 0, core, chip].reshape(256, 512), late[l, 1, core, chip].reshape(256, 512)
+        part = mm(keys, attn_weight(l, 1), NT) + mm(values, attn_weight(l, 2), NT)
+        dx[l, chip] = part.astype(BF).reshape(2, 128, 512)
+        return send(dx.at[l, chip, peer], dx_near.at[l, chip], "dx", (l, (chip + x_lo) % 2), near)
+
+    def give_far(l, copy):
         copy.wait_recv()
-        span = slice(256 * part, 256 * part + 256)
-        mine = dkv[l, 1 - x_lo, core, :, :, span].astype(F32) + dkv_near[l, 1 - x_lo, :, :, span].astype(F32)
-        dkv[l, 1 - x_lo, core, :, :, span] = mine.astype(BF)
-        return send(
-            dkv.at[l, 1 - x_lo, core, :, :, halves(part)], dkv_far.at[l, :, :, halves(part)], "dkv", (l, part, 1), across
-        )
+        mine = dx[l, 1 - x_lo, core].astype(F32) + dx_near[l, 1 - x_lo].astype(F32)
+        dx[l, 1 - x_lo, core] = mine.astype(BF)
+        return send(dx.at[l, 1 - x_lo, core], dx_far.at[l], "dx", (l, 2), across)
 
     def act_arrive(l, which):
         if which == 3:
@@ -516,6 +534,27 @@
 
     def two(ref, *index):
         return ref[index].reshape(256, -1)
+
+    def mlp_grads(l, got_second):
+        got_second.wait_recv()
+        act_arrive(l, 2)
+        act_arrive(l, 3)
+        theirs = r["du"].at[l, core, peer]
+        remote(theirs, theirs, r["back_send"].at[l, 1], r["back_recv"].at[l, 1], near).wait_recv()
+        put_grad(l, 1, 0, two(pairs, l, 2), lambda low, high: r["du"][l, core, :, :, low:high].reshape(256, -1), 2)
+        put_grad(l, 1, 1, two(pairs, l, 3), lambda low, high: r["act"][l, core, :, :, low:high].reshape(256, -1), 2)
+        scatter.step(l, 1, 0)
+
+    s4, fin, total = r["s4"], r["fin"], r["total"]
+    moved = []
+
+    def hand_out(l):
+        for dst in range(4):
+            s4[dst, l] = total[l, 4 * dst : 4 * dst + 4, :]
+        for step in (1, 2, 3):
+            member, device = place.in_group(step)
+            moved.append(send(s4.at[member, l], fin.at[seq, l], "a2a", (l, step), device))
+        fin[seq, l] = s4[seq, l]
 
     grad = r["cotangent"][...].astype(F32)
     for l in (1, 0):
@@ -537,8 +576,6 @@
             grad_normed = grad_normed + mm(grad_pre, weight(l, 1, half, low, low + 512), NT)
         mine = r["du"].at[l, peer, core]
         send(mine, mine, "back", (l, 1), near)
-        if l == 0:
-            scatter.step(1, 1, 1)
         hat = r["hat1"][l]
         put_row(l, 3, column_sum(grad_normed * hat))
         put_row(l, 4, column_sum(grad_normed))
@@ -547,90 +584,83 @@
         low_first = grad_first.astype(BF)
         early[l, 1, core] = low_first
         grad_mixed = mm(low_first, attn_weight(l, 3), NT).astype(BF)
-        near_ways, far_ways = [], []
+        if l == 0:
+            scatter.step(1, 1, 1)
+            mlp_grads(0, got_second)
         for pair in range(4):
             low = 128 * pair
             keys, values = group_rows(l, 0, low), group_rows(l, 1, low)
             grad_pair = both(grad_mixed[:, low : low + 128])
             probs = r["probs"][l, pair]
             grad_probs = mm(grad_pair, values, NT)
-            dkv[l, :, :, 1, :, low : low + 128] = mm(probs, grad_pair, TN).astype(BF).reshape(2, 2, 128, 128)
+            late[l, 1, core, :, :, low : low + 128] = mm(probs, grad_pair, TN).astype(BF).reshape(2, 256, 128)
             wide = probs.astype(F32)
             row_dot = jnp.sum(grad_probs * wide, axis=-1, keepdims=True)
             grad_scores = (wide * (grad_probs - row_dot)).astype(BF)
             early[l, 0, core, :, low : low + 128] = (joined(mm(grad_scores, keys)) * SCALE).astype(BF)
             grad_keys = mm(grad_scores, both(r["q"][l, :, low : low + 128]), TN) * SCALE
-            dkv[l, :, :, 0, :, low : low + 128] = grad_keys.astype(BF).reshape(2, 2, 128, 128)
-            if pair % 2 == 1:
-                near_ways.append(give_near(l, pair // 2))
-            if pair == 2:
-                far_ways.append(give_far(l, 0, near_ways[0]))
+            late[l, 0, core, :, :, low : low + 128] = grad_keys.astype(BF).reshape(2, 256, 128)
+            if l == 0 and pair == 1:
+                scatter.step(1, 0, 1)
+        mine = late.at[l, peer, core]
+        send(mine, mine, "back", (l, 3), near)
         mine = early.at[l, peer, core]
         send(mine, mine, "back", (l, 2), near)
         grad_queries = early[l, 0, core]
         put_row(l, 0, column_sum(grad_queries.astype(F32)))
+        put_row(l, 1, column_sum(late[l, 1, core].reshape(512, 512).astype(F32)))
+        if l == 0:
+            for y in range(4):
+                r["vtab"][y] = vgrad[:, 128 * y : 128 * y + 128]
+            table = Table(place, r["vtab"], r["vgot"].at[1], r["v_send"].at[1], r["v_recv"].at[1])
+            table.start("y", "collect")
+
+        def attn_grads():
+            act_arrive(l, 1)
+            theirs = early.at[l, core, peer]
+            remote(theirs, theirs, r["back_send"].at[l, 2], r["back_recv"].at[l, 2], near).wait_recv()
+            put_grad(l, 0, 0, two(pairs, l, core), lambda low, high: two(early, l, core), 1)
+            theirs = late.at[l, core, peer]
+            remote(theirs, theirs, r["back_send"].at[l, 3], r["back_recv"].at[l, 3], near).wait_recv()
+            rows = xall[l].reshape(512, 512)
+            value = mm(rows, late[l, core, 0].reshape(512, 512), TN) + mm(rows, late[l, core, 1].reshape(512, 512), TN)
+            ga[l, 1] = value.astype(BF).reshape(4, 2, 4, 16, 512)
+            scatter.step(l, 0, 0)
+
+        if l == 0:
+            attn_grads()
+        far_near = grad_rows(l, 1 - x_lo)
+        own_near = grad_rows(l, x_lo)
+        far_way = give_far(l, far_near)
         grad = grad_first + mm(grad_queries, attn_weight(l, 0), NT)
-        far_ways.append(give_far(l, 1, near_ways[1]))
-        if l == 0:
-            scatter.step(1, 0, 1)
-        got_second.wait_recv()
-        act_arrive(l, 2)
-        act_arrive(l, 3)
-        theirs = r["du"].at[l, core, peer]
-        remote(theirs, theirs, r["back_send"].at[l, 1], r["back_recv"].at[l, 1], near).wait_recv()
-        put_grad(l, 1, 0, two(pairs, l, 2), lambda low, high: r["du"][l, core, :, :, low:high].reshape(256, -1), 2)
-        put_grad(l, 1, 1, two(pairs, l, 3), lambda low, high: r["act"][l, core, :, :, low:high].reshape(256, -1), 2)
-        scatter.step(l, 1, 0)
-        act_arrive(l, 0)
-        act_arrive(l, 1)
-        theirs = early.at[l, core, peer]
-        remote(theirs, theirs, r["back_send"].at[l, 2], r["back_recv"].at[l, 2], near).wait_recv()
-        put_grad(l, 0, 0, two(pairs, l, core), lambda low, high: two(early, l, core), 1)
-        if l == 0:
+        if l == 1:
+            mlp_grads(1, got_second)
+            attn_grads()
+        else:
             scatter.step(1, 1, 2)
             scatter.step(1, 0, 2)
-        for copy in far_ways:
-            copy.wait_recv()
-        for which in range(2):
-            total = dkv[l, x_lo, core, which].astype(F32) + dkv_near[l, x_lo, which].astype(F32)
-            late[l, which, core] = (total + dkv_far[l, which].astype(F32)).astype(BF)
-        mine = late.at[l, peer, core]
-        send(mine, mine, "back", (l, 3), near)
-        put_row(l, 1, column_sum(late[l, 1, core].astype(F32)))
-        if l == 0:
-            table = Table(place, vgrad, r["vgot"].at[1], r["v_send"].at[1], r["v_recv"].at[1])
-            table.start(0)
-        grad = grad + mm(late[l, 0, core], attn_weight(l, 1), NT) + mm(late[l, 1, core], attn_weight(l, 2), NT)
-        theirs = late.at[l, core, peer]
-        remote(theirs, theirs, r["back_send"].at[l, 3], r["back_recv"].at[l, 3], near).wait_recv()
-        put_grad(l, 0, 1, two(pairs, l, 0), lambda low, high: two(late, l, core), 1)
-        if l == 0:
-            table.finish(0)
-            table.start(1)
-        scatter.step(l, 0, 0)
+            table.finish()
+            table.start("x")
+            scatter.step(0, 1, 1)
+            scatter.step(1, 1, 3)
+            scatter.step(1, 0, 3)
+            hand_out(1)
+        own_near.wait_recv()
+        far_way.wait_recv()
+        grad = grad + dx[l, x_lo, core].astype(F32) + dx_near[l, x_lo].astype(F32) + dx_far[l].astype(F32)
     r["input_grad"][...] = grad
-    scatter.step(1, 1, 3)
-    scatter.step(1, 0, 3)
-    table.finish(1)
-    table.start(2)
-    scatter.step(0, 1, 1)
     scatter.step(0, 0, 1)
-    table.finish(2)
-    table.start(3)
+    table.finish()
+    table.start("z")
     scatter.step(0, 1, 2)
     scatter.step(0, 0, 2)
-    table.finish(3)
+    table.finish()
+    table.start("core")
     scatter.step(0, 1, 3)
     scatter.step(0, 0, 3)
-    s4, fin, total = r["s4"], r["fin"], r["total"]
-    for dst in range(4):
-        for l in range(2):
-            s4[dst, l] = total[l, 4 * dst : 4 * dst + 4, :]
-    moved = []
-    for step in (1, 2, 3):
-        member, device = place.in_group(step)
-        moved.append(send(s4.at[member], fin.at[seq], "a2a", (1, step), device))
-    fin[seq] = s4[seq]
+    hand_out(0)
+    table.finish()
+    r["vfin"][...] = pltpu.roll(r["vtab"][place.at["y"]], (128 - 4 * (number % 32)) % 128, 1)
     gather.finish()
     scatter.finish()
     for copy in moved:
@@ -639,12 +669,12 @@
         copy.wait_send()
 
 
-INPUTS = ("tokens", "cotangent", "seg_row", "seg_col", "w_attn", "w_mlp", "table")
+INPUTS = ("tokens", "cotangent", "segments", "w_attn", "w_mlp", "vectors")
 OUTPUTS = {
     "block_out": ((128, 512), BF),
     "input_grad": ((128, 512), F32),
     "fin": ((4, 2, 4, 1536), F32),
-    "vgrad": ((24, 512), F32),
+    "vfin": ((24, 128), F32),
 }
 DIMS = (2, 2, 2, 4, 2, 4, 16)
 HALF = (2, 2, 4, 2, 4, 16)
@@ -654,39 +684,44 @@
     "ga": (HALF + (512,), BF),
     "gm": (HALF + (1024,), BF),
     "vec": ((24, 512), F32),
-    "s0": ((4, 2, 4, 1536), F32),
-    "r0": ((4, 2, 4, 1536), F32),
+    "vgrad": ((24, 512), F32),
+    "tab": ((4, 24, 128), F32),
+    "vtab": ((4, 24, 128), F32),
+    "t0": ((4, 16, 768), F32),
+    "s0": ((4, 16, 768), BF),
+    "r0": ((4, 16, 768), BF),
     "s4": ((4, 2, 4, 1536), F32),
     "stage": ((2, 16, 1536), F32),
     "total": ((2, 16, 1536), F32),
-    "vgot": ((2, 4, 3, 24, 512), F32),
+    "vgot": ((2, 4, 3, 24, 128), F32),
     "docs": ((4, 1, 128), jnp.int32),
     "bias": ((128, 512), F32),
     "q": ((2, 128, 512), BF),
-    "kv": ((2, 4, 2, 128, 512), BF),
+    "kv": ((2, 2, 2, 256, 512), BF),
+    "xall": ((2, 2, 2, 128, 512), BF),
     "probs": ((2, 4, 256, 512), BF),
     "pairs": ((2, 4, 2, 128, 512), BF),
     "act": ((2, 2, 2, 128, 1024), BF),
     "du": ((2, 2, 2, 128, 1024), BF),
     "early": ((2, 2, 2, 128, 512), BF),
-    "late": ((2, 2, 2, 128, 512), BF),
+    "late": ((2, 2, 2, 2, 256, 512), BF),
     "hat1": ((2, 128, 512), F32),
     "inv1": ((2, 128, 1), F32),
     "slope": ((2, 128, 2048), BF),
     "hat2": ((2, 128, 512), F32),
     "inv2": ((2, 128, 1), F32),
-    "dkv": ((2, 2, 2, 2, 128, 512), BF),
-    "dkv_near": ((2, 2, 2, 128, 512), BF),
-    "dkv_far": ((2, 2, 128, 512), BF),
+    "dx": ((2, 2, 2, 128, 512), BF),
+    "dx_near": ((2, 2, 128, 512), BF),
+    "dx_far": ((2, 128, 512), BF),
 }
 SEMS = {
-    "a2a": (2, 4),
+    "a2a": (3, 4),
     "doc": (4,),
     "ag": (2, 2, 3, 3, 3),
     "sw": (2, 2, 3, 4),
     "rs": (2, 2, 3, 3, 3),
-    "kv": (2, 2, 3),
-    "dkv": (2, 2, 2),
+    "x": (2, 3),
+    "dx": (2, 3),
     "act": (2, 4),
     "back": (2, 4),
     "v": (2, 4, 3),
@@ -729,28 +764,44 @@
     return (first_new, second_new, weight_new)
 
 
+def adam_kernel(block_in, grad_in, fin, vfin, *refs):
+    state, (block_out, grad_out), outs = refs[:9], refs[9:11], refs[11:]
+    block_out[...] = block_in[...]
+    grad_out[...] = grad_in[...]
+    for l in range(2):
+        for arr in range(3):
+            w, m, v = state[arr], state[3 + arr], state[6 + arr]
+            if arr == 2:
+                pieces = [(vfin[12 * l : 12 * l + 12, 0:4], slice(0, 4))]
+            elif arr == 1:
+                pieces = [(fin[s, l, :, 512:1536], slice(1024 * s, 1024 * s + 1024)) for s in range(4)]
+            else:
+                pieces = [(fin[s, l, :, 0:512], slice(512 * q, 512 * q + 512)) for s, q in enumerate(QUARTERS)]
+            rate, decay = (VECTOR_RATE, 0.0) if arr == 2 else (LEARN_RATE, WEIGHT_DECAY)
+            for grad, span in pieces:
+                new = adam_update(w[l, :, span], grad, m[l, :, span], v[l, :, span], rate, decay)
+                for k in range(3):
+                    outs[3 * arr + k][l, :, span] = new[k]
+
+
+def adam(block, grad, fin, vfin, *state):
+    shapes = [jax.ShapeDtypeStruct(a.shape, a.dtype) for a in (block, grad)]
+    for a in state[:3]:
+        shapes += [jax.ShapeDtypeStruct(a.shape, a.dtype)] * 3
+    spec = pl.BlockSpec(memory_space=pltpu.VMEM)
+    return pl.pallas_call(
+        adam_kernel, out_shape=shapes, in_specs=[spec] * 13, out_specs=[spec] * 11, name="adam"
+    )(block, grad, fin, vfin, *state)
+
+
 def local(
     tokens, cotangent, segments, w_attn, w_mlp, vectors, m_attn, m_mlp, m_vec, v_attn, v_mlp, v_vec
 ):
-    place = lax.axis_index("dp") * 4 + lax.axis_index("seq")
-    table = lax.dynamic_update_slice(
-        jnp.zeros((24, 512), F32),
-        vectors.astype(BF).astype(F32).reshape(24, 4),
-        (0, 4 * place),
+    made = train(tokens[0], cotangent[0], segments, w_attn, w_mlp, vectors)
+    block_out, input_grad, *updated = adam(
+        *made, w_attn, w_mlp, vectors, m_attn, m_mlp, m_vec, v_attn, v_mlp, v_vec
     )
-    block_out, input_grad, fin, vec_total = train(
-        tokens[0], cotangent[0], segments, segments.reshape(128, 1), w_attn, w_mlp, table
-    )
-    grad_attn = jnp.concatenate([fin[QUARTERS.index(q), ..., :512] for q in range(4)], axis=-1)
-    grad_mlp = fin[..., 512:].transpose(1, 2, 0, 3).reshape(2, 4, 4096)
-    grad_vec = lax.dynamic_slice(vec_total, (0, 4 * place), (24, 4)).reshape(2, 12, 4)
-    return (
-        block_out[None],
-        input_grad[None],
-        *adam_update(w_attn, grad_attn, m_attn, v_attn, LEARN_RATE, WEIGHT_DECAY),
-        *adam_update(w_mlp, grad_mlp, m_mlp, v_mlp, LEARN_RATE, WEIGHT_DECAY),
-        *adam_update(vectors, grad_vec, m_vec, v_vec, VECTOR_RATE, 0.0),
-    )
+    return (block_out[None], input_grad[None], *updated)
 
 
 def solution(mesh):

time: 146 us -> 121 us (0.83)
  Pallas kernels: 135 us -> 115 us
  other arithmetic: 2.32 us -> 0 us
    pallas_call x1, Pallas kernels: 135 us -> 113 us  [train(): pl.pallas_call(train_kernel, out_shape=tuple((jax.ShapeDtypeStruct(*spec)...]
    sub x3 -> x0, other arithmetic: 2.32 us -> none  [adam_update(): weight - rate * (first_new / first_fix / (jnp.sqrt(second_new / second_fi...]
    pallas_call x0 -> x1, Pallas kernels: none -> 2.29 us  [adam(): pl.pallas_call(adam_kernel, out_shape=shapes, in_specs=[spec] * 13, out_s...]
    unnamed x31 -> x16, local copies, waits for them, and re-layouts: 3.82 us -> 5.53 us
where the time goes in v3:
time: 121 us
  Pallas kernels  115 us (95%)
  local copies, waits for them, and re-layouts  5.53 us (5%)
    pallas_call x1, Pallas kernels, train(): pl.pallas_call(train_kernel, out_shape=tuple((jax.ShapeDtypeStruct(*spec)...  113 us
    unnamed x16, local copies, waits for them, and re-layouts  5.53 us

profile of v3, /device:TPU:1, one launch (start us, length us, event | category | flops | bytes accessed | tf_op | source)
XLA Modules:
  0.0 121.1 jit_solution(15297684508108469553)
XLA Ops:
  0.6 0.0 copy-start.3
  0.7 1.4 %copy.23.refs_5_.refs_2_ = f32[2,12,4]{2,1,0:T(8,128)} copy(f32[2,12,4]{1,2,0:T(4,128)} %param.17) | data formatting | bytes 768 | tf_op args[5]
  2.0 0.0 copy-done.3
  2.0 0.0 copy-start.4
  2.0 0.7 copy.25.refs_5_
  2.7 0.0 copy-done.4
  2.7 0.7 copy.26.refs_8_
  3.4 112.6 %train.1 = (bf16[128,512]{1,0:T(8,128)(2,1)}, f32[128,512]{1,0:T(8,128)}, f32[4,2,4,1536]{3,2,1,0:T(4,128)}, f32[24,128]{1,0:T(8,128)}) custom-call(bf16[128,512]{1,0:T(8,128)(2,1)} %bitcast.4, bf16[128,512]{1,0:T(8,128)(2,1)} %bitcast.5, s32[1,128]{1,0:T(1,128)} %refs_2_.2, f32[2,4,2048]{2,1,0:T(4,128)} %refs_0_.1, f32[2,4,4096]{2,1,0:T(4,128)} %refs_1_.1, ...), custom_call_target="tpu_custom_call" | custom-call | tf_op jit(solution)/shard_map/train/pallas_call | solution.py:743
  116.0 2.3 %adam.1 = (bf16[128,512]{1,0:T(8,128)(2,1)}, f32[128,512]{1,0:T(8,128)}, f32[2,4,2048]{2,1,0:T(4,128)}, f32[2,4,2048]{2,1,0:T(4,128)}, f32[2,4,2048]{2,1,0:T(4,1...) custom-call(bf16[128,512]{1,0:T(8,128)(2,1)} %get-tuple-element.26.b, ...), custom_call_target="tpu_custom_call" | custom-call | tf_op jit(solution)/shard_map/adam/pallas_call | solution.py:792
  118.3 0.0 copy-start.2
  118.3 0.0 copy-start.1
  118.3 0.7 copy-done.2
  119.0 0.0 copy-start
  119.0 0.7 copy.27
  119.7 0.0 copy-done.1
  119.7 0.7 copy.28
  120.4 0.0 copy-done
  120.4 0.7 copy.29
Async XLA Ops:
  0.6 1.4 %copy-start.3 = (f32[2,12,4]{1,2,0:T(4,128)S(1)}, f32[2,12,4]{1,2,0:T(4,128)}, u32[]{:S(2)}) copy-start(f32[2,12,4]{1,2,0:T(4,128)} %param.20) | copy-start | bytes 1156
  2.0 0.7 copy-start.4
  118.3 0.7 copy-start.2
  118.3 1.4 %copy-start.1 = (f32[2,12,4]{2,1,0:T(8,128)S(1)}, f32[2,12,4]{2,1,0:T(8,128)}, u32[]{:S(2)}) copy-start(f32[2,12,4]{2,1,0:T(8,128)} %get-tuple-element.50) | copy-start | bytes 1156
  119.0 1.4 %copy-start = (f32[2,12,4]{2,1,0:T(8,128)S(1)}, f32[2,12,4]{2,1,0:T(8,128)}, u32[]{:S(2)}) copy-start(f32[2,12,4]{2,1,0:T(8,128)} %get-tuple-element.51) | copy-start | bytes 1156

commit v4 on v3

--- a/solution.py
+++ b/solution.py
@@ -20,7 +20,9 @@
 MESH = pl.DeviceIdType.MESH
 BF = jnp.bfloat16
 F32 = jnp.float32
-THIRDS = (((0, 128), (128, 256), (256, 512)), ((0, 384), (384, 768), (768, 1024)))
+EVEN = (((0, 128), (128, 256), (256, 512)), ((0, 384), (384, 768), (768, 1024)))
+UNEVEN = (((0, 256), (256, 384), (384, 512)), ((0, 384), (384, 640), (640, 1024)))
+THIRDS = (EVEN, UNEVEN)
 WIDTHS = (512, 1024)
 ORDERS = (("x", "y", "z"), ("y", "z", "x"), ("z", "x", "y"))
 
@@ -75,7 +77,7 @@
     peers.append(far)
     for peer in peers:
         pl.semaphore_signal(barrier, inc=1, device_id=peer, device_id_type=MESH)
-    pl.semaphore_wait(barrier, len(peers))
+    return barrier, len(peers)
 
 
 def remote(src, dst, send, recv, device):
@@ -196,7 +198,7 @@
                 spot = dict(here)
                 if coming:
                     spot[axis] = (place.at[axis] - step) % 4
-                ref = region(self.bufs[arr], l, spot, place.core, THIRDS[arr][j])
+                ref = region(self.bufs[arr], l, spot, place.core, THIRDS[l][arr][j])
                 sems = (self.send.at[l, arr, phase, j, step - 1], self.recv.at[l, arr, phase, j, step - 1])
                 out.append(remote(ref, ref, *sems, device))
         return out
@@ -216,7 +218,7 @@
         place = self.place
         axis = ORDERS[j][2]
         core = 1 - place.core if coming else place.core
-        ref = region(self.bufs[arr], l, {axis: (place.at[axis] - step) % 4}, core, THIRDS[arr][j])
+        ref = region(self.bufs[arr], l, {axis: (place.at[axis] - step) % 4}, core, THIRDS[l][arr][j])
         return remote(
             ref, ref, self.swap_send.at[l, arr, j, step], self.swap_recv.at[l, arr, j, step], place.other_core()
         )
@@ -247,13 +249,13 @@
     def __init__(self, place, bufs, slots, total, send, recv):
         self.place, self.bufs, self.slots, self.total, self.send, self.recv = place, bufs, slots, total, send, recv
 
-    def slot(self, phase, arr, j):
-        return self.slots[(phase * 2 + arr) * 3 + j]
+    def slot(self, l, phase, arr, j):
+        return self.slots[((l * 3 + phase) * 2 + arr) * 3 + j]
 
     def part(self, l, arr, at, j):
         whole = slice(None)
         x_hi, x_lo = (at["x"] // 2, at["x"] % 2) if "x" in at else (whole, whole)
-        low, high = THIRDS[arr][j]
+        low, high = THIRDS[l][arr][j]
         return self.bufs[arr].at[
             l, x_lo, at.get("y", whole), x_hi, at.get("z", whole), whole, pl.ds(low, high - low)
         ]
@@ -266,7 +268,7 @@
             for step in (1, 2, 3):
                 there = {a: place.at[a] for a in rev[:phase]}
                 there[rev[phase]], device = place.along(rev[phase], step)
-                dst = self.slot(phase, arr, j).at[l, step - 1]
+                dst = self.slot(l, phase, arr, j).at[step - 1]
                 sems = (self.send.at[l, arr, phase, j, step - 1], self.recv.at[l, arr, phase, j, step - 1])
                 out.append(remote(self.part(l, arr, there, j), dst, *sems, device))
         return out
@@ -275,19 +277,19 @@
         for j, order in enumerate(ORDERS):
             rev = order[::-1]
             own = self.part(l, arr, {a: self.place.at[a] for a in rev[: phase + 1]}, j)
-            came = self.slot(phase, arr, j)
+            came = self.slot(l, phase, arr, j)
             if phase == 2:
-                low, high = THIRDS[arr][j]
+                low, high = THIRDS[l][arr][j]
                 total = own[...].astype(F32)
                 for k in range(3):
-                    total = total + came[l, k].astype(F32)
+                    total = total + came[k].astype(F32)
                 self.total[l, :, 512 * arr + low : 512 * arr + high] = total
                 continue
 
             def body(index, own=own, came=came):
                 total = own[index].astype(F32)
                 for k in range(3):
-                    total = total + came[(l, k) + index].astype(F32)
+                    total = total + came[(k,) + index].astype(F32)
                 own[index] = total.astype(BF)
 
             each_block(dims_of(rev[phase + 1 :]), body)
@@ -326,6 +328,7 @@
         unsent.append(copy)
         return copy
 
+    greeted = greet(place)
     t0 = r["t0"]
     for s, q in enumerate(QUARTERS):
         for l in range(2):
@@ -335,14 +338,16 @@
     s0[...] = t0[...].astype(BF)
     tab = r["tab"]
     number = place.dp * 4 + seq
-    tab[place.at["y"]] = jnp.zeros((24, 128), F32)
+    square = r["square"]
+    square[...] = jnp.zeros((128, 128), F32)
     for l in range(2):
-        tab[place.at["y"], 12 * l : 12 * l + 12, 0:4] = r["vectors"][l].astype(BF).astype(F32)
+        square[0:4, 0:12] = r["vectors"][l].astype(BF).astype(F32)
+        tab[place.at["y"], 12 * l : 12 * l + 12, :] = square[...].T[0:12, :]
     tab[place.at["y"]] = pltpu.roll(tab[place.at["y"]], 4 * (number % 32), 1)
     r["docs"][seq] = r["segments"][...]
     xall = r["xall"]
     xall[0, x_lo, core] = r["tokens"][...]
-    greet(place)
+    pl.semaphore_wait(*greeted)
 
     pieces, docs = [], []
     for step in (1, 2, 3):
@@ -381,18 +386,21 @@
         came = xall.at[l, 1 - x_lo, core]
         return send(came, came, "x", (l, 2), near)
 
-    first_near, first_far = share(0)
-    table.finish()
-    table.start("z")
-    for chunk in CHUNKS:
+    for chunk in CHUNKS[:2]:
         gather.arrive(*chunk, 0)
         gather.start(*chunk, 1)
     table.finish()
+    table.start("z")
+    gather.arrive(0, 0, 1)
+    gather.start(0, 0, 2)
+    table.finish()
     table.start("y", "spread")
-    for chunk in CHUNKS[:2]:
-        gather.arrive(*chunk, 1)
-        gather.start(*chunk, 2)
-    first_on = pass_on(0, first_far)
+    first_near, first_far = share(0)
+    gather.arrive(0, 1, 1)
+    gather.start(0, 1, 2)
+    for chunk in CHUNKS[2:]:
+        gather.arrive(*chunk, 0)
+        gather.start(*chunk, 1)
     for copy in docs:
         copy.wait_recv()
     own_docs = jnp.broadcast_to(r["docs"][seq].astype(F32), (128, 128)).T
@@ -402,6 +410,7 @@
     for y in range(4):
         vec[:, 128 * y : 128 * y + 128] = tab[y]
     gather.swap_start(0, 0)
+    first_on = pass_on(0, first_far)
     for chunk in CHUNKS[2:]:
         gather.arrive(*chunk, 1)
         gather.start(*chunk, 2)
@@ -660,7 +669,10 @@
     scatter.step(0, 0, 3)
     hand_out(0)
     table.finish()
-    r["vfin"][...] = pltpu.roll(r["vtab"][place.at["y"]], (128 - 4 * (number % 32)) % 128, 1)
+    r["vtab"][place.at["y"]] = pltpu.roll(r["vtab"][place.at["y"]], (128 - 4 * (number % 32)) % 128, 1)
+    for l in range(2):
+        square[0:12, :] = r["vtab"][place.at["y"], 12 * l : 12 * l + 12, :]
+        r["vfin"][l] = square[...].T[0:8, :]
     gather.finish()
     scatter.finish()
     for copy in moved:
@@ -674,7 +686,7 @@
     "block_out": ((128, 512), BF),
     "input_grad": ((128, 512), F32),
     "fin": ((4, 2, 4, 1536), F32),
-    "vfin": ((24, 128), F32),
+    "vfin": ((2, 8, 128), F32),
 }
 DIMS = (2, 2, 2, 4, 2, 4, 16)
 HALF = (2, 2, 4, 2, 4, 16)
@@ -688,6 +700,7 @@
     "tab": ((4, 24, 128), F32),
     "vtab": ((4, 24, 128), F32),
     "t0": ((4, 16, 768), F32),
+    "square": ((128, 128), F32),
     "s0": ((4, 16, 768), BF),
     "r0": ((4, 16, 768), BF),
     "s4": ((4, 2, 4, 1536), F32),
@@ -731,12 +744,13 @@
 
 def train(*args):
     slots = []
-    for phase in range(3):
-        for arr in range(2):
-            for j in range(3):
-                low, high = THIRDS[arr][j]
-                rest = dims_of(ORDERS[j][::-1][phase + 1 :])
-                slots.append(pltpu.VMEM((2, 3) + rest + (16, high - low), BF))
+    for l in range(2):
+        for phase in range(3):
+            for arr in range(2):
+                for j in range(3):
+                    low, high = THIRDS[l][arr][j]
+                    rest = dims_of(ORDERS[j][::-1][phase + 1 :])
+                    slots.append(pltpu.VMEM((3,) + rest + (16, high - low), BF))
     scratch = [pltpu.VMEM(*spec) for spec in SCRATCH.values()]
     for shape in SEMS.values():
         scratch += [pltpu.SemaphoreType.DMA(shape)] * 2
@@ -772,7 +786,7 @@
         for arr in range(3):
             w, m, v = state[arr], state[3 + arr], state[6 + arr]
             if arr == 2:
-                pieces = [(vfin[12 * l : 12 * l + 12, 0:4], slice(0, 4))]
+                pieces = [(vfin[l, 0:4, 0:12], slice(0, 12))]
             elif arr == 1:
                 pieces = [(fin[s, l, :, 512:1536], slice(1024 * s, 1024 * s + 1024)) for s in range(4)]
             else:
@@ -797,11 +811,12 @@
 def local(
     tokens, cotangent, segments, w_attn, w_mlp, vectors, m_attn, m_mlp, m_vec, v_attn, v_mlp, v_vec
 ):
+    vectors, m_vec, v_vec = (a.transpose(0, 2, 1) for a in (vectors, m_vec, v_vec))
     made = train(tokens[0], cotangent[0], segments, w_attn, w_mlp, vectors)
     block_out, input_grad, *updated = adam(
         *made, w_attn, w_mlp, vectors, m_attn, m_mlp, m_vec, v_attn, v_mlp, v_vec
     )
-    return (block_out[None], input_grad[None], *updated)
+    return (block_out[None], input_grad[None], *updated[:6], *(a.transpose(0, 2, 1) for a in updated[6:]))
 
 
 def solution(mesh):

time: 121 us -> 116 us (0.959)
  local copies, waits for them, and re-layouts: 5.53 us -> 0 us
    unnamed x16 -> x0, local copies, waits for them, and re-layouts: 5.53 us -> none
where the time goes in v4:
time: 116 us
  Pallas kernels  116 us (100%)
    pallas_call x1, Pallas kernels, train(): pl.pallas_call(train_kernel, out_shape=tuple((jax.ShapeDtypeStruct(*spec)...  113 us

profile of v4, /device:TPU:1, one launch (start us, length us, event | category | flops | bytes accessed | tf_op | source)
XLA Modules:
  0.0 116.3 jit_solution(7794903575999359744)
XLA Ops:
  0.6 113.2 %train.1 = (bf16[128,512]{1,0:T(8,128)(2,1)}, f32[128,512]{1,0:T(8,128)}, f32[4,2,4,1536]{3,2,1,0:T(4,128)}, f32[2,8,128]{2,1,0:T(8,128)}) custom-call(bf16[128,512]{1,0:T(8,128)(2,1)} %bitcast.10, bf16[128,512]{1,0:T(8,128)(2,1)} %bitcast.11, s32[1,128]{1,0:T(1,128)} %refs_2_.1, f32[2,4,2048]{2,1,0:T(4,128)} %refs_0_.1, f32[2,4,4096]{2,1,0:T(4,128)} %refs_1_.1, ...), custom_call_target="tpu_custom_call" | custom-call | tf_op jit(solution)/shard_map/train/pallas_call | solution.py:757
  113.9 2.3 %adam.1 = (bf16[128,512]{1,0:T(8,128)(2,1)}, f32[128,512]{1,0:T(8,128)}, f32[2,4,2048]{2,1,0:T(4,128)}, f32[2,4,2048]{2,1,0:T(4,128)}, f32[2,4,2048]{2,1,0:T(4,1...) custom-call(bf16[128,512]{1,0:T(8,128)(2,1)} %get-tuple-element.26.b, ...), custom_call_target="tpu_custom_call" | custom-call | tf_op jit(solution)/shard_map/adam/pallas_call | solution.py:806

commit v5 on v4

--- a/solution.py
+++ b/solution.py
@@ -358,6 +358,17 @@
     for step in (1, 2, 3):
         member, device = place.in_group(step)
         docs.append(send(r["docs"].at[seq], r["docs"].at[seq], "doc", step, device))
+    def share(l):
+        mine = xall.at[l, x_lo, core]
+        near_way = send(mine, mine, "x", (l, 0), near)
+        return near_way, send(mine, mine, "x", (l, 1), across)
+
+    def pass_on(l, far_way):
+        far_way.wait_recv()
+        came = xall.at[l, 1 - x_lo, core]
+        return send(came, came, "x", (l, 2), near)
+
+    first_near, first_far = share(0)
     r0[seq] = s0[seq]
     for copy in pieces:
         copy.wait_recv()
@@ -376,26 +387,16 @@
     for chunk in CHUNKS:
         gather.start(*chunk, 0)
 
-    def share(l):
-        mine = xall.at[l, x_lo, core]
-        near_way = send(mine, mine, "x", (l, 0), near)
-        return near_way, send(mine, mine, "x", (l, 1), across)
-
-    def pass_on(l, far_way):
-        far_way.wait_recv()
-        came = xall.at[l, 1 - x_lo, core]
-        return send(came, came, "x", (l, 2), near)
-
     for chunk in CHUNKS[:2]:
         gather.arrive(*chunk, 0)
         gather.start(*chunk, 1)
     table.finish()
     table.start("z")
+    first_on = pass_on(0, first_far)
     gather.arrive(0, 0, 1)
     gather.start(0, 0, 2)
     table.finish()
     table.start("y", "spread")
-    first_near, first_far = share(0)
     gather.arrive(0, 1, 1)
     gather.start(0, 1, 2)
     for chunk in CHUNKS[2:]:
@@ -410,7 +411,6 @@
     for y in range(4):
         vec[:, 128 * y : 128 * y + 128] = tab[y]
     gather.swap_start(0, 0)
-    first_on = pass_on(0, first_far)
     for chunk in CHUNKS[2:]:
         gather.arrive(*chunk, 1)
         gather.start(*chunk, 2)
@@ -546,12 +546,12 @@
 
     def mlp_grads(l, got_second):
         got_second.wait_recv()
+        act_arrive(l, 3)
+        put_grad(l, 1, 1, two(pairs, l, 3), lambda low, high: r["act"][l, core, :, :, low:high].reshape(256, -1), 2)
         act_arrive(l, 2)
-        act_arrive(l, 3)
         theirs = r["du"].at[l, core, peer]
         remote(theirs, theirs, r["back_send"].at[l, 1], r["back_recv"].at[l, 1], near).wait_recv()
         put_grad(l, 1, 0, two(pairs, l, 2), lambda low, high: r["du"][l, core, :, :, low:high].reshape(256, -1), 2)
-        put_grad(l, 1, 1, two(pairs, l, 3), lambda low, high: r["act"][l, core, :, :, low:high].reshape(256, -1), 2)
         scatter.step(l, 1, 0)
 
     s4, fin, total = r["s4"], r["fin"], r["total"]
@@ -585,6 +585,9 @@
             grad_normed = grad_normed + mm(grad_pre, weight(l, 1, half, low, low + 512), NT)
         mine = r["du"].at[l, peer, core]
         send(mine, mine, "back", (l, 1), near)
+        if l == 0:
+            scatter.step(1, 1, 1)
+        mlp_grads(l, got_second)
         hat = r["hat1"][l]
         put_row(l, 3, column_sum(grad_normed * hat))
         put_row(l, 4, column_sum(grad_normed))
@@ -593,9 +596,6 @@
         low_first = grad_first.astype(BF)
         early[l, 1, core] = low_first
         grad_mixed = mm(low_first, attn_weight(l, 3), NT).astype(BF)
-        if l == 0:
-            scatter.step(1, 1, 1)
-            mlp_grads(0, got_second)
         for pair in range(4):
             low = 128 * pair
             keys, values = group_rows(l, 0, low), group_rows(l, 1, low)
@@ -643,7 +643,6 @@
         far_way = give_far(l, far_near)
         grad = grad_first + mm(grad_queries, attn_weight(l, 0), NT)
         if l == 1:
-            mlp_grads(1, got_second)
             attn_grads()
         else:
             scatter.step(1, 1, 2)

time: 116 us -> 113 us (0.974)
  Pallas kernels: 116 us -> 112 us
    pallas_call x1, Pallas kernels: 113 us -> 110 us  [train(): pl.pallas_call(train_kernel, out_shape=tuple((jax.ShapeDtypeStruct(*spec)...]
where the time goes in v5:
time: 113 us
  Pallas kernels  112 us (99%)
    pallas_call x1, Pallas kernels, train(): pl.pallas_call(train_kernel, out_shape=tuple((jax.ShapeDtypeStruct(*spec)...  110 us
    pallas_call x1, Pallas kernels, adam(): pl.pallas_call(adam_kernel, out_shape=shapes, in_specs=[spec] * 13, out_s...  2.28 us

profile of v5, /device:TPU:1, one launch (start us, length us, event | category | flops | bytes accessed | tf_op | source)
XLA Modules:
  0.0 113.2 jit_solution(7310815870675591239)
XLA Ops:
  0.6 110.1 %train.1 = (bf16[128,512]{1,0:T(8,128)(2,1)}, f32[128,512]{1,0:T(8,128)}, f32[4,2,4,1536]{3,2,1,0:T(4,128)}, f32[2,8,128]{2,1,0:T(8,128)}) custom-call(bf16[128,512]{1,0:T(8,128)(2,1)} %bitcast.10, bf16[128,512]{1,0:T(8,128)(2,1)} %bitcast.11, s32[1,128]{1,0:T(1,128)} %refs_2_.1, f32[2,4,2048]{2,1,0:T(4,128)} %refs_0_.1, f32[2,4,4096]{2,1,0:T(4,128)} %refs_1_.1, ...), custom_call_target="tpu_custom_call" | custom-call | tf_op jit(solution)/shard_map/train/pallas_call | solution.py:756
  110.7 2.3 %adam.1 = (bf16[128,512]{1,0:T(8,128)(2,1)}, f32[128,512]{1,0:T(8,128)}, f32[2,4,2048]{2,1,0:T(4,128)}, f32[2,4,2048]{2,1,0:T(4,128)}, f32[2,4,2048]{2,1,0:T(4,1...) custom-call(bf16[128,512]{1,0:T(8,128)(2,1)} %get-tuple-element.26.b, ...), custom_call_target="tpu_custom_call" | custom-call | tf_op jit(solution)/shard_map/adam/pallas_call | solution.py:805

commit v6 on v5

--- a/solution.py
+++ b/solution.py
@@ -583,10 +583,10 @@
             put_row(l, 5 + i, column_sum(grad_pre.astype(F32)))
             r["du"][l, half, core, :, low : low + 512] = grad_pre
             grad_normed = grad_normed + mm(grad_pre, weight(l, 1, half, low, low + 512), NT)
+            if l == 0 and i == 1:
+                scatter.step(1, 1, 1)
         mine = r["du"].at[l, peer, core]
         send(mine, mine, "back", (l, 1), near)
-        if l == 0:
-            scatter.step(1, 1, 1)
         mlp_grads(l, got_second)
         hat = r["hat1"][l]
         put_row(l, 3, column_sum(grad_normed * hat))
@@ -649,10 +649,10 @@
             scatter.step(1, 0, 2)
             table.finish()
             table.start("x")
-            scatter.step(0, 1, 1)
             scatter.step(1, 1, 3)
             scatter.step(1, 0, 3)
             hand_out(1)
+            scatter.step(0, 1, 1)
         own_near.wait_recv()
         far_way.wait_recv()
         grad = grad + dx[l, x_lo, core].astype(F32) + dx_near[l, x_lo].astype(F32) + dx_far[l].astype(F32)

time: 113 us -> 115 us (1.018)
  Pallas kernels: 112 us -> 114 us
    pallas_call x1, Pallas kernels: 110 us -> 112 us  [train(): pl.pallas_call(train_kernel, out_shape=tuple((jax.ShapeDtypeStruct(*spec)...]
where the time goes in v6:
time: 115 us
  Pallas kernels  114 us (99%)
    pallas_call x1, Pallas kernels, train(): pl.pallas_call(train_kernel, out_shape=tuple((jax.ShapeDtypeStruct(*spec)...  112 us

profile of v6, /device:TPU:1, one launch (start us, length us, event | category | flops | bytes accessed | tf_op | source)
XLA Modules:
  0.0 114.8 jit_solution(5331424879018560643)
XLA Ops:
  0.6 111.7 %train.1 = (bf16[128,512]{1,0:T(8,128)(2,1)}, f32[128,512]{1,0:T(8,128)}, f32[4,2,4,1536]{3,2,1,0:T(4,128)}, f32[2,8,128]{2,1,0:T(8,128)}) custom-call(bf16[128,512]{1,0:T(8,128)(2,1)} %bitcast.10, bf16[128,512]{1,0:T(8,128)(2,1)} %bitcast.11, s32[1,128]{1,0:T(1,128)} %refs_2_.1, f32[2,4,2048]{2,1,0:T(4,128)} %refs_0_.1, f32[2,4,4096]{2,1,0:T(4,128)} %refs_1_.1, ...), custom_call_target="tpu_custom_call" | custom-call | tf_op jit(solution)/shard_map/train/pallas_call | solution.py:756
  112.3 2.3 %adam.1 = (bf16[128,512]{1,0:T(8,128)(2,1)}, f32[128,512]{1,0:T(8,128)}, f32[2,4,2048]{2,1,0:T(4,128)}, f32[2,4,2048]{2,1,0:T(4,128)}, f32[2,4,2048]{2,1,0:T(4,1...) custom-call(bf16[128,512]{1,0:T(8,128)(2,1)} %get-tuple-element.26.b, ...), custom_call_target="tpu_custom_call" | custom-call | tf_op jit(solution)/shard_map/adam/pallas_call | solution.py:805
